TPU v7x, 256 devices: a whole 4x4x8 slice. The times are simulated.
256 devices in a mesh: row: 8 (over x_lo, y), col: 32 (over z, x_hi, core).
Axes of the slice: x: 4 (x_hi: 2, x_lo: 2; x = x_hi * 2 + x_lo), y: 4, z: 8, core: 2. Of those that a mesh axis runs over, the one named last changes fastest.
Arguments:
- row_emb: float32 [32, 512, 256], P('row', 'col'), may hold values from -1.8 to 1.8
- col_emb: float32 [128, 512, 256], P('col', 'row'), may hold values from -1.8 to 1.8
- row_marg: bfloat16 [32, 512], P('row', 'col'), may hold values from 0.5 to 3
- col_marg: bfloat16 [128, 512], P('col', 'row'), may hold values from 0.5 to 3
- tile_list: int32 [8, 32, 8, 2], P('row', 'col'), may hold values from 0 to 127, as said below
- tile_count: int32 [8, 32], P('row', 'col'), may hold values from 1 to 8, as said below
- tile_data: int32 [8, 32, 8, 512, 512], P('row', 'col'), may hold values from 0 to 215
Outputs:
- row_new: float32 [32, 512, 256], P('row', 'col')
- col_new: float32 [128, 512, 256], P('col', 'row')
Inputs may be any that keep to these rules, and one draw needn't show every extreme that they name: `tile_list`: the slots of device (r, c) name distinct tiles with row block in r * 4 to (r + 1) * 4 - 1 and column block in c * 4 to (c + 1) * 4 - 1; slots at or past the device's tile_count are not used. `tile_count`: some device uses all 8 slots.
All inputs are finite; a program needn't handle non-finite values.
Results may differ from a plain program's by a relative error of at most 0.012.
Values may be sent and summed in bfloat16 or wider, within the bound.
A program may use at most 64 MiB of HBM per device.

v0:
```python
import jax
import jax.numpy as jnp
from jax import lax
from jax.sharding import PartitionSpec as P


def tile_signal(scores, counts, marg_left, marg_right):
    level = counts.astype(jnp.float32)
    diff = scores - (jnp.log(jnp.maximum(level, 1.0)) - marg_left[:, None] - marg_right[None, :])
    weight = 0.1 + 0.25 * jnp.sqrt(level)
    return jnp.where(level > 0.0, weight * diff, jax.nn.sigmoid(diff))


def accumulate(
    row_panel, col_panel, marg_rows, marg_cols, listing, used_slots, tile_block, row_base, col_base
):

    def one_tile(slot_index, carry):
        grad_rows, grad_cols = carry
        i = listing[slot_index, 0] - row_base
        j = listing[slot_index, 1] - col_base
        row_piece = lax.dynamic_index_in_dim(row_panel, i, 0, keepdims=False)
        col_piece = lax.dynamic_index_in_dim(col_panel, j, 0, keepdims=False)
        scores = lax.dot_general(
            row_piece, col_piece, (((1,), (1,)), ((), ())), preferred_element_type=jnp.float32
        )
        counts = lax.dynamic_index_in_dim(tile_block, slot_index, 0, keepdims=False)
        marg_left = lax.dynamic_index_in_dim(marg_rows, i, 0, keepdims=False)
        marg_right = lax.dynamic_index_in_dim(marg_cols, j, 0, keepdims=False)
        signal = tile_signal(scores, counts, marg_left, marg_right).astype(jnp.bfloat16)
        row_term = jnp.dot(signal, col_piece, preferred_element_type=jnp.float32)
        col_term = lax.dot_general(
            signal, row_piece, (((0,), (0,)), ((), ())), preferred_element_type=jnp.float32
        )
        old_row = lax.dynamic_index_in_dim(grad_rows, i, 0, keepdims=False)
        old_col = lax.dynamic_index_in_dim(grad_cols, j, 0, keepdims=False)
        grad_rows = lax.dynamic_update_index_in_dim(grad_rows, old_row + row_term, i, 0)
        grad_cols = lax.dynamic_update_index_in_dim(grad_cols, old_col + col_term, j, 0)
        return (grad_rows, grad_cols)

    start = (jnp.zeros(row_panel.shape, jnp.float32), jnp.zeros(col_panel.shape, jnp.float32))
    return lax.fori_loop(0, used_slots, one_tile, start)


def shards(row_emb, col_emb, row_marg, col_marg, tile_list, tile_count, tile_data):
    row_base = lax.axis_index("row") * row_emb.shape[0]
    col_base = lax.axis_index("col") * col_emb.shape[0]
    listing = tile_list[0, 0]
    used_slots = tile_count[0, 0]
    tile_block = tile_data[0, 0]
    for substep in range(2):
        col_panel, marg_cols = (
            lax.all_gather(col_emb.astype(jnp.bfloat16), "row", axis=1, tiled=True),
            lax.all_gather(col_marg, "row", axis=1, tiled=True),
        )
        marg_cols = marg_cols.astype(jnp.float32)
        row_panel, marg_half = (
            lax.all_gather(row_emb.astype(jnp.bfloat16), "col", axis=1, tiled=True),
            lax.all_gather(row_marg, "col", axis=1, tiled=True),
        )
        marg_rows = marg_half.astype(jnp.float32)
        grad_rows, grad_cols = accumulate(
            row_panel,
            col_panel,
            marg_rows,
            marg_cols,
            listing,
            used_slots,
            tile_block,
            row_base,
            col_base,
        )
        col_share = lax.psum_scatter(
            grad_cols.astype(jnp.bfloat16), "row", scatter_dimension=1, tiled=True
        ).astype(jnp.float32)
        col_emb = col_emb - 0.0004 * col_share
        own_share = lax.psum_scatter(
            grad_rows.astype(jnp.bfloat16), "col", scatter_dimension=1, tiled=True
        ).astype(jnp.float32)
        row_emb = row_emb - 0.0004 * own_share
    return (row_emb, col_emb)


def solution(mesh):
    placed = (
        P("row", "col", None),
        P("col", "row", None),
        P("row", "col"),
        P("col", "row"),
        P("row", "col", None, None),
        P("row", "col"),
        P("row", "col", None, None, None),
    )
    return jax.shard_map(
        shards,
        mesh=mesh,
        in_specs=placed,
        out_specs=(P("row", "col", None), P("col", "row", None)),
        check_vma=False,
    )
```

profile of v0, /device:TPU:1, one launch (start us, length us, event | category | flops | bytes accessed | tf_op | source)
XLA Modules:
  0.0 697.6 jit_solution(11643285170313549713)
XLA Ops:
  7.2 1.6 convert_element_type.59
  10.4 16.6 %all-gather.1 = bf16[8,64,4]{1,2,0:T(4,128)(2,1)S(1)} all-gather(bf16[1,64,4]{1,2,0:T(4,128)(2,1)} %bitcast.182), channel_id=1, replica_groups=mesh['row'=8,'col'=32] {'row'}, dimensions={0}, use_global_device_ids=true | all-gather | bytes 4608 | tf_op jit(solution)/shard_map/all_gather | solution.py:54
  27.1 48.6 %all-gather = bf16[32,16,4]{1,2,0:T(4,128)(2,1)S(1)} all-gather(bf16[1,16,4]{1,2,0:T(4,128)(2,1)} %bitcast.183), channel_id=1, replica_groups=mesh['row'=8,'col'=32] {'col'}, dimensions={0}, use_global_device_ids=true | all-gather | bytes 4224 | tf_op jit(solution)/shard_map/all_gather | solution.py:59
  76.1 54.3 %all-gather.7.cloned.1.call-done = bf16[4,512,256]{2,1,0:T(8,128)(2,1)} async-done(((bf16[4,16,256]{2,1,0:T(8,128)(2,1)}), bf16[4,512,256]{2,1,0:T(8,128)(2,1)}) %all-gather.7.cloned.1.call-update) | async-done | bytes 1048592 | tf_op jit(solution)/shard_map/all_gather | solution.py:58
  130.6 1.5 broadcast.53.clone.1
  132.1 17.4 %while.24 = (s32[]{:T(128)}, f32[4,512,256]{2,1,0:T(8,128)}, f32[4,512,256]{2,1,0:T(8,128)S(1)}, s32[]{:T(128)}, s32[8,2]{0,1:T(2,128)S(1)}, /*index=5*/s32[]{:T...) while((s32[]{:T(128)}, f32[4,512,256]{2,1,0:T(8,128)}, ...), condition=%wide.region_1.2_spmd, body=%wide.region_0.1_spmd.sunk | while | flops 406585344 | bytes 7876955 | solution.py:42
  134.7 2.3 fusion.68
  143.1 2.3 fusion.68
  149.5 2.7 convert_element_type.62
  153.5 153.2 %reduce-scatter.5.cloned.1.call-done = bf16[4,16,256]{2,1,0:T(8,128)(2,1)} async-done(((bf16[4,512,256]{2,1,0:T(8,128)(2,1)}), bf16[4,16,256]{2,1,0:T(8,128)(2,1)}) %reduce-scatter.5.cloned.1.call-update) | async-done | bytes 32784 | tf_op jit(solution)/shard_map/reduce_scatter | solution.py:77
  308.2 41.3 %reduce-scatter.7.cloned.1.call-done = bf16[4,64,256]{2,1,0:T(8,128)(2,1)} async-done(((bf16[4,512,256]{2,1,0:T(8,128)(2,1)}), bf16[4,64,256]{2,1,0:T(8,128)(2,1)}) %reduce-scatter.7.cloned.1.call-update) | async-done | bytes 131088 | tf_op jit(solution)/shard_map/reduce_scatter | solution.py:73
  349.4 1.6 fusion.38
  351.1 77.8 %all-gather.11.cloned.1.call-done = bf16[4,512,256]{2,1,0:T(8,128)(2,1)} async-done(((bf16[4,16,256]{2,1,0:T(8,128)(2,1)}), bf16[4,512,256]{2,1,0:T(8,128)(2,1)}) %all-gather.11.cloned.1.call-update) | async-done | bytes 1048592 | tf_op jit(solution)/shard_map/all_gather | solution.py:58
  428.9 36.3 %all-gather.13.cloned.1.call-done = bf16[4,512,256]{2,1,0:T(8,128)(2,1)} async-done(((bf16[4,64,256]{2,1,0:T(8,128)(2,1)}), bf16[4,512,256]{2,1,0:T(8,128)(2,1)}) %all-gather.13.cloned.1.call-update) | async-done | bytes 1048592 | tf_op jit(solution)/shard_map/all_gather | solution.py:53
  465.4 1.5 broadcast.53
  466.9 17.4 %while.25 = (s32[]{:T(128)}, f32[4,512,256]{2,1,0:T(8,128)}, f32[4,512,256]{2,1,0:T(8,128)S(1)}, s32[]{:T(128)}, s32[8,2]{0,1:T(2,128)S(1)}, /*index=5*/s32[]{:T...) while((s32[]{:T(128)}, f32[4,512,256]{2,1,0:T(8,128)}, ...), condition=%wide.region_5.6_spmd, body=%wide.region_4.5_spmd.sunk | while | flops 406585344 | bytes 7876955 | solution.py:42
  469.5 2.3 fusion.77
  472.9 2.1 fusion.78
  477.8 2.3 fusion.77
  481.2 2.0 fusion.78
  484.3 2.7 convert_element_type.68
  488.2 158.3 %reduce-scatter.9.cloned.1.call-done = bf16[4,16,256]{2,1,0:T(8,128)(2,1)} async-done(((bf16[4,512,256]{2,1,0:T(8,128)(2,1)}), bf16[4,16,256]{2,1,0:T(8,128)(2,1)}) %reduce-scatter.9.cloned.1.call-update) | async-done | bytes 32784 | tf_op jit(solution)/shard_map/reduce_scatter | solution.py:77
  647.9 41.1 %reduce-scatter.11.cloned.1.call-done = bf16[4,64,256]{2,1,0:T(8,128)(2,1)} async-done(((bf16[4,512,256]{2,1,0:T(8,128)(2,1)}), bf16[4,64,256]{2,1,0:T(8,128)(2,1)}) %reduce-scatter.11.cloned.1.call-update) | async-done | bytes 131088 | tf_op jit(solution)/shard_map/reduce_scatter | solution.py:73
  689.1 1.7 multiply_subtract_fusion
  (61 shorter events, 20.0 us)
Async XLA Ops:
  7.2 68.9 %all-gather.9.cloned.1.call-start = ((), (), s32[]{:S(2)}) async-start(), calls=%async_computation.5 | async-start | bytes 1179648 | tf_op jit(solution)/shard_map/all_gather | solution.py:53
  8.9 121.6 %all-gather.7.cloned.1.call-start = ((), (), s32[]{:S(2)}) async-start(), calls=%async_computation.4 | async-start | bytes 1081344 | tf_op jit(solution)/shard_map/all_gather | solution.py:58
  10.4 296.3 %reduce-scatter.5.cloned.1.call-start = ((), (), s32[]{:S(2)}) async-start(), calls=%async_computation.6 | async-start | bytes 1081344 | tf_op jit(solution)/shard_map/reduce_scatter | solution.py:77
  130.4 1.7 copy-start.1
  130.4 1.7 copy-start.6
  152.2 197.2 %reduce-scatter.7.cloned.1.call-start = ((), (), s32[]{:S(2)}) async-start(), calls=%async_computation.8 | async-start | bytes 1179648 | tf_op jit(solution)/shard_map/reduce_scatter | solution.py:73
  152.3 154.4 %copy-start.3 = (f32[4,16,256]{2,1,0:T(8,128)S(1)}, f32[4,16,256]{2,1,0:T(8,128)}, u32[]{:S(2)}) copy-start(f32[4,16,256]{2,1,0:T(8,128)} %param.11) | copy-start | bytes 196612
  152.3 197.1 %copy-start = (f32[4,64,256]{2,1,0:T(8,128)S(1)}, f32[4,64,256]{2,1,0:T(8,128)}, u32[]{:S(2)}) copy-start(f32[4,64,256]{2,1,0:T(8,128)} %param.12) | copy-start | bytes 786436
  153.4 275.5 %all-gather.11.cloned.1.call-start = ((), (), s32[]{:S(2)}) async-start(), calls=%async_computation.7 | async-start | bytes 1081344 | tf_op jit(solution)/shard_map/all_gather | solution.py:58
  308.1 157.1 %all-gather.13.cloned.1.call-start = ((), (), s32[]{:S(2)}) async-start(), calls=%async_computation.9 | async-start | bytes 1179648 | tf_op jit(solution)/shard_map/all_gather | solution.py:53
  351.0 295.5 %reduce-scatter.9.cloned.1.call-start = ((), (), s32[]{:S(2)}) async-start(), calls=%async_computation.10 | async-start | bytes 1081344 | tf_op jit(solution)/shard_map/reduce_scatter | solution.py:77
  428.9 38.0 %copy-start.2 = (bf16[4,512,256]{2,1,0:T(8,128)(2,1)S(1)}, bf16[4,512,256]{2,1,0:T(8,128)(2,1)}, u32[]{:S(2)}) copy-start(bf16[4,512,256]{2,1,0:T(8,128)(2,1)} %all-gather.11.cloned.1.call-done) | copy-start | bytes 3145732
  487.0 202.1 %reduce-scatter.11.cloned.1.call-start = ((), (), s32[]{:S(2)}) async-start(), calls=%async_computation.11 | async-start | bytes 1179648 | tf_op jit(solution)/shard_map/reduce_scatter | solution.py:73
  487.0 159.5 %copy-start.5 = (bf16[4,16,256]{2,1,0:T(8,128)(2,1)S(1)}, bf16[4,16,256]{2,1,0:T(8,128)(2,1)}, u32[]{:S(2)}) copy-start(bf16[4,16,256]{2,1,0:T(8,128)(2,1)} %reduce-scatter.5.cloned.1.call-done) | copy-start | bytes 98308
  487.1 202.0 %copy-start.4 = (bf16[4,64,256]{2,1,0:T(8,128)(2,1)S(1)}, bf16[4,64,256]{2,1,0:T(8,128)(2,1)}, u32[]{:S(2)}) copy-start(bf16[4,64,256]{2,1,0:T(8,128)(2,1)} %reduce-scatter.7.cloned.1.call-done) | copy-start | bytes 393220
Sparse Core Ops, SparseCore 0:
  10.4 40.5 all-gather.8
  54.1 76.2 all-gather.6
  152.3 154.3 reduce-scatter.4
  309.2 40.1 reduce-scatter.6
  352.7 76.1 all-gather.10
  431.3 33.9 all-gather.12
  487.1 159.3 reduce-scatter.8
  649.1 39.9 reduce-scatter.10
where the time goes:
time: 704 us; the launch traced here: 698 us
  waiting for transfers between devices  563 us (80%)
  blocking collectives  65.2 us (9%)
  matrix products  18.6 us (3%)
  other arithmetic  16.7 us (2%)
  between operations  14.2 us (2%)
  local copies, waits for them, and re-layouts  10.6 us (2%)
  loops' own time  9.3 us (1%)
    reduce_scatter x2, waiting for transfers between devices, shards(): lax.psum_scatter(grad_rows.astype(jnp.bfloat16), 'col', scatter_dimension...  312 us
    all_gather x2, waiting for transfers between devices, shards(): lax.all_gather(row_emb.astype(jnp.bfloat16), 'col', axis=1, tiled=True)  132 us
    reduce_scatter x2, waiting for transfers between devices, shards(): lax.psum_scatter(grad_cols.astype(jnp.bfloat16), 'row', scatter_dimension...  82.4 us
    all_gather x1, blocking collectives, shards(): lax.all_gather(row_marg, 'col', axis=1, tiled=True)  48.6 us
    all_gather x2, waiting for transfers between devices, shards(): lax.all_gather(col_emb.astype(jnp.bfloat16), 'row', axis=1, tiled=True)  36.3 us
    all_gather x1, blocking collectives, shards(): lax.all_gather(col_marg, 'row', axis=1, tiled=True)  16.6 us
  transfers between devices with their start and end apart: 8, of which 7 were waited for; matrix products, arithmetic and copies ran while one was open for 1% of the time, Pallas kernels for 0%

commit v1 on v0

v1 whole, which is shorter than its diff:
```python
import jax
import jax.numpy as jnp
from jax import lax
from jax.experimental import pallas as pl
from jax.experimental.pallas import tpu as pltpu
from jax.sharding import PartitionSpec as P

MESH = pl.DeviceIdType.MESH
BF16, F32 = jnp.bfloat16, jnp.float32
B, K = 512, 256
SLOTS = 8
NY = 4
NROW = 8
NZ = 8
NZX = 16
ROWS, COLS = 16, 64
CHUNK = 256


def place(q):
    n = q // 2
    odd = lax.rem(n, 2)
    dz = lax.rem(odd * ((n + 1) // 2) + (1 - odd) * (NZ - n // 2), NZ)
    return dz, lax.rem(q, 2)


def kernel(
    count_ref, list_ref, row_ref, col_ref, rowm_ref, colm_ref, data_ref, row_out, col_out,
    row_panel, col_panel, row_marg, col_marg, marg_left, marg_right, minus_log, weight,
    stage, row_term, col_term, row_send, row_half, row_sum, row_got, col_send, col_got, slot_of, pair_of,
    data_sem, rp_s, rp_r, rf_s, rf_r, cp_s, cp_r, rm_s, rm_r, rmf_s, rmf_r, cm_s, cm_r,
    sib_s, sib_r, rg_s, rg_r, cg_s, cg_r,
):
    r, c = lax.axis_index("row"), lax.axis_index("col")
    xl, y = r // NY, lax.rem(r, NY)
    zx, core = c // 2, lax.rem(c, 2)
    z, xh = zx // 2, lax.rem(zx, 2)
    sibling = {"row": r, "col": zx * 2 + (1 - core)}

    def to_zx(q):
        dz, dx = place(q)
        return lax.rem(z + dz, NZ) * 2 + lax.rem(xh + dx, 2)

    def from_zx(q):
        dz, dx = place(q)
        return lax.rem(z - dz + NZ, NZ) * 2 + lax.rem(xh + dx, 2)

    def zx_device(t):
        return {"row": r, "col": t * 2 + core}

    def to_row(q):
        return lax.rem(xl + q // NY, 2) * NY + lax.rem(y + lax.rem(q, NY), NY)

    def from_row(q):
        return lax.rem(xl + q // NY, 2) * NY + lax.rem(y - lax.rem(q, NY) + NY, NY)

    def row_device(t):
        return {"row": t, "col": c}

    def copy(src, dst, send, recv, device):
        return pltpu.make_async_remote_copy(
            src_ref=src, dst_ref=dst, send_sem=send, recv_sem=recv, device_id=device, device_id_type=MESH
        )

    def loop(lo, hi, body):
        def step(i, carry):
            body(i)
            return carry

        lax.fori_loop(lo, hi, step, 0)

    barrier = pltpu.get_barrier_semaphore()

    def greet_zx(q):
        pl.semaphore_signal(barrier, inc=1, device_id=zx_device(to_zx(q)), device_id_type=MESH)

    def greet_row(q):
        pl.semaphore_signal(barrier, inc=1, device_id=row_device(to_row(q)), device_id_type=MESH)

    loop(1, NZX, greet_zx)
    loop(1, NROW, greet_row)
    pl.semaphore_signal(barrier, inc=1, device_id=sibling, device_id_type=MESH)

    def data_copy(s):
        return pltpu.make_async_copy(data_ref.at[0, 0, s], stage.at[s], data_sem.at[s])

    loop(0, SLOTS, lambda s: data_copy(s).start())

    row_out[...] = row_ref[...]
    col_out[...] = col_ref[...]
    row_marg[c] = rowm_ref[...]
    col_marg[r] = colm_ref[...]
    row_term[SLOTS] = jnp.zeros((B, K), F32)
    col_term[SLOTS] = jnp.zeros((B, K), F32)

    codes = []
    for s in range(SLOTS):
        i = jnp.clip(list_ref[s, 0] - r * 4, 0, 3)
        j = jnp.clip(list_ref[s, 1] - c * 4, 0, 3)
        pair_of[s, 0] = i
        pair_of[s, 1] = j
        codes.append(jnp.where(s < count_ref[0], i * 4 + j, -1))
    for pair in range(16):
        found = jnp.int32(SLOTS)
        for s in range(SLOTS):
            found = jnp.where(codes[s] == pair, s, found)
        slot_of[pair] = found

    def row_panel_send(p, q):
        mine = row_panel.at[p, c]
        return copy(mine, mine, rp_s.at[p, q], rp_r.at[p, q], zx_device(to_zx(q)))

    def row_panel_recv(p, q):
        t = from_zx(q)
        got = row_panel.at[p, t * 2 + core]
        return copy(got, got, rp_s.at[p, q], rp_r.at[p, q], zx_device(t))

    def row_panel_hand(p, q):
        got = row_panel.at[p, from_zx(q) * 2 + core]
        return copy(got, got, rf_s.at[p, q], rf_r.at[p, q], sibling)

    def row_panel_handed(p, q):
        got = row_panel.at[p, from_zx(q) * 2 + (1 - core)]
        return copy(got, got, rf_s.at[p, q], rf_r.at[p, q], sibling)

    def col_panel_send(p, q):
        mine = col_panel.at[p, r]
        return copy(mine, mine, cp_s.at[p, q], cp_r.at[p, q], row_device(to_row(q)))

    def col_panel_recv(p, q):
        t = from_row(q)
        got = col_panel.at[p, t]
        return copy(got, got, cp_s.at[p, q], cp_r.at[p, q], row_device(t))

    def col_panel_pass(p, q):
        got = col_panel.at[p, (1 - xl) * NY + y]
        return copy(got, got, cp_s.at[p, q], cp_r.at[p, q], row_device(to_row(q - NY)))

    def row_marg_send(q):
        mine = row_marg.at[c]
        return copy(mine, mine, rm_s.at[q], rm_r.at[q], zx_device(to_zx(q)))

    def row_marg_recv(q):
        t = from_zx(q)
        got = row_marg.at[t * 2 + core]
        return copy(got, got, rm_s.at[q], rm_r.at[q], zx_device(t))

    def col_marg_send(q):
        mine = col_marg.at[r]
        return copy(mine, mine, cm_s.at[q], cm_r.at[q], row_device(to_row(q)))

    def col_marg_recv(q):
        t = from_row(q)
        got = col_marg.at[t]
        return copy(got, got, cm_s.at[q], cm_r.at[q], row_device(t))

    def gather_start(p):
        col_panel[p, r] = col_out[...].astype(BF16)
        row_panel[p, c] = row_out[...].astype(BF16)

    def row_gather_send(p):
        loop(1, NZX, lambda q: row_panel_send(p, NZX - q).start())
        row_panel_hand(p, 0).start()

    def col_gather_send(p):
        col_panel_send(p, NY).start()
        loop(1, NY, lambda q: col_panel_send(p, q).start())

    def hand_on(p, q):
        row_panel_recv(p, q).wait_recv()
        row_panel_hand(p, q).start()

    def pass_on(p):
        col_panel_recv(p, NY).wait_recv()
        loop(NY + 1, NROW, lambda q: col_panel_pass(p, q).start())

    def gather_end(p):
        loop(1, NY, lambda q: col_panel_recv(p, q).wait_recv())
        loop(NY + 1, NROW, lambda q: col_panel_recv(p, q).wait_recv())
        loop(0, NZX, lambda q: row_panel_handed(p, q).wait_recv())

    def gather_sent(p):
        loop(1, NZX, lambda q: row_panel_send(p, q).wait_send())
        loop(0, NZX, lambda q: row_panel_hand(p, q).wait_send())
        loop(1, NROW, lambda q: col_panel_send(p, q).wait_send())

    gather_start(0)
    pl.semaphore_wait(barrier, NZX - 1 + NROW - 1 + 1)
    col_gather_send(0)
    row_gather_send(0)
    loop(1, NROW, lambda q: col_marg_send(q).start())
    loop(1, NZX, lambda q: row_marg_send(q).start())

    def prepare(s):
        data_copy(s).wait()

        def part(h, carry):
            rows = pl.ds(pl.multiple_of(h * 64, 64), 64)
            level = stage[s, rows].astype(F32)
            minus_log[s, rows] = -jnp.log(jnp.maximum(level, 1.0)).astype(BF16)
            weight[s, rows] = jnp.where(level > 0.0, 0.1 + 0.25 * jnp.sqrt(level), 0.0).astype(BF16)
            return carry

        lax.fori_loop(0, B // 64, part, 0)

    def prepare_and_hand(s):
        prepare(s)
        hand_on(0, 2 * s + 1)

        @pl.when(s < SLOTS - 1)
        def _():
            hand_on(0, 2 * s + 2)

    loop(0, 3, prepare_and_hand)
    pass_on(0)
    loop(3, SLOTS, prepare_and_hand)

    loop(1, NROW, lambda q: col_marg_recv(q).wait_recv())
    loop(1, NZX, lambda q: row_marg_recv(q).wait_recv())

    def marg_pass(q):
        got = row_marg.at[from_zx(q) * 2 + core]
        return copy(got, got, rmf_s.at[q], rmf_r.at[q], sibling)

    def marg_passed(q):
        got = row_marg.at[from_zx(q) * 2 + (1 - core)]
        return copy(got, got, rmf_s.at[q], rmf_r.at[q], sibling)

    loop(0, NZX, lambda q: marg_pass(q).start())
    loop(0, NZX, lambda q: marg_passed(q).wait_recv())

    gather_end(0)
    spread = row_marg[...].reshape(B, 128)
    lane = lax.broadcasted_iota(jnp.int32, (B, 128), 1)
    place_in = lax.rem(lax.broadcasted_iota(jnp.int32, (B, 128), 0), ROWS)
    ones = jnp.ones((128, 128), BF16)
    for i in range(4):
        picked = jnp.where(lane == i * ROWS + place_in, spread.astype(F32), 0.0).astype(BF16)
        marg_left[i] = jnp.dot(picked, ones, preferred_element_type=F32)
    low = lax.broadcasted_iota(jnp.int32, (16, 128), 1) < COLS
    for g in range(NROW // 2):
        marg_right[:, g * 128 : (g + 1) * 128] = jnp.where(
            low, col_marg[2 * g].astype(F32), col_marg[2 * g + 1].astype(F32)
        )

    def tiles(p):
        def tile(s):
            i, j = pair_of[s, 0], pair_of[s, 1]
            col_piece = col_panel[p, :, j].reshape(B, K)
            row_piece = row_panel[p, :, i].reshape(B, K)
            right = marg_right[pl.ds(j, 1), :]
            total = None
            for h in range(B // CHUNK):
                rows = slice(h * CHUNK, (h + 1) * CHUNK)
                mine = row_piece[rows]
                left = marg_left[i, rows, :]
                scores = lax.dot_general(mine, col_piece, (((1,), (1,)), ((), ())), preferred_element_type=F32)
                left = jnp.concatenate([left] * (B // 128), axis=1)
                diff = scores + (minus_log[s, rows].astype(F32) + right) + left
                scale = weight[s, rows].astype(F32)
                signal = jnp.where(scale > 0.0, scale * diff, 0.5 * jnp.tanh(0.5 * diff) + 0.5).astype(BF16)
                row_term[s, rows] = jnp.dot(signal, col_piece, preferred_element_type=F32)
                part = lax.dot_general(signal, mine, (((0,), (0,)), ((), ())), preferred_element_type=F32)
                total = part if total is None else total + part
            col_term[s] = total

        loop(0, SLOTS, tile)

    def sibling_send(p):
        return copy(row_send.at[1 - core], row_half.at[p], sib_s.at[p], sib_r.at[p], sibling)

    def row_grad_send(p, q):
        t = to_zx(q)
        return copy(row_sum.at[t], row_got.at[p, q], rg_s.at[p, q], rg_r.at[p, q], zx_device(t))

    def col_grad_send(p, q):
        t = to_row(q)
        return copy(col_send.at[t], col_got.at[p, q], cg_s.at[p, q], cg_r.at[p, q], row_device(t))

    def scatter_start(p):
        def row_part(t):
            for k in range(2):
                rows = pl.ds(pl.multiple_of(t * 32 + k * ROWS, ROWS), ROWS)
                for i in range(4):
                    found = [row_term[slot_of[i * 4 + j], rows, :] for j in range(4)]
                    row_send[k, t, i] = ((found[0] + found[1]) + (found[2] + found[3])).astype(BF16)

        loop(0, NZX, row_part)
        sibling_send(p).start()

        def col_part(t):
            for part in range(2):
                rows = pl.ds(pl.multiple_of(t * COLS + part * 32, 32), 32)
                for j in range(4):
                    found = [col_term[slot_of[i * 4 + j], rows, :] for i in range(4)]
                    col_send[t, j, part * 32 : part * 32 + 32] = (
                        (found[0] + found[1]) + (found[2] + found[3])
                    ).astype(BF16)

        loop(0, NROW, col_part)
        loop(1, NROW, lambda q: col_grad_send(p, NROW - q).start())
        sibling_send(p).wait_recv()

        def add(t):
            row_sum[t] = (row_send[core, t].astype(F32) + row_half[p, t].astype(F32)).astype(BF16)

        loop(0, NZX, add)
        loop(1, NZX, lambda q: row_grad_send(p, NZX - q).start())

    def col_update(p):
        loop(1, NROW, lambda q: col_grad_send(p, q).wait_recv())
        for j in range(4):
            total = col_send[r, j].astype(F32)
            for q in range(1, NROW):
                total = total + col_got[p, q, j].astype(F32)
            col_out[j] = col_out[j] - 0.0004 * total

    def row_update(p):
        loop(1, NZX, lambda q: row_grad_send(p, q).wait_recv())
        total = row_sum[zx].astype(F32)
        for q in range(1, NZX):
            total = total + row_got[p, q].astype(F32)
        row_out[...] = row_out[...] - 0.0004 * total

    def scatter_sent(p):
        loop(1, NROW, lambda q: col_grad_send(p, q).wait_send())
        loop(1, NZX, lambda q: row_grad_send(p, q).wait_send())
        sibling_send(p).wait_send()

    tiles(0)
    scatter_start(0)
    col_update(0)
    col_panel[1, r] = col_out[...].astype(BF16)
    col_gather_send(1)
    row_update(0)
    row_panel[1, c] = row_out[...].astype(BF16)
    row_gather_send(1)
    pass_on(1)
    loop(1, NZX, lambda q: hand_on(1, q))
    scatter_sent(0)
    gather_end(1)
    tiles(1)
    scatter_start(1)
    col_update(1)
    row_update(1)
    scatter_sent(1)
    gather_sent(0)
    gather_sent(1)
    loop(1, NROW, lambda q: col_marg_send(q).wait_send())
    loop(1, NZX, lambda q: row_marg_send(q).wait_send())
    loop(0, NZX, lambda q: marg_pass(q).wait_send())


def shards(row_emb, col_emb, row_marg, col_marg, tile_list, tile_count, tile_data):
    rowm = jnp.broadcast_to(jnp.pad(row_marg.reshape(1, 64), ((0, 0), (0, 64))), (16, 128))
    colm = jnp.tile(col_marg, (4, 2))
    vmem = pl.BlockSpec(memory_space=pltpu.VMEM)
    smem = pl.BlockSpec(memory_space=pltpu.SMEM)
    dma = pltpu.SemaphoreType.DMA
    return pl.pallas_call(
        kernel,
        out_shape=(
            jax.ShapeDtypeStruct(row_emb.shape, F32),
            jax.ShapeDtypeStruct(col_emb.shape, F32),
        ),
        in_specs=[smem, smem, vmem, vmem, vmem, vmem, pl.BlockSpec(memory_space=pl.ANY)],
        out_specs=(vmem, vmem),
        scratch_shapes=[
            pltpu.VMEM((2, 32, 4, ROWS, K), BF16),
            pltpu.VMEM((2, NROW, 4, COLS, K), BF16),
            pltpu.VMEM((32, 16, 128), BF16),
            pltpu.VMEM((NROW, 16, 128), BF16),
            pltpu.VMEM((4, B, 128), F32),
            pltpu.VMEM((16, B), F32),
            pltpu.VMEM((SLOTS, B, B), BF16),
            pltpu.VMEM((SLOTS, B, B), BF16),
            pltpu.VMEM((SLOTS, B, B), jnp.int32),
            pltpu.VMEM((SLOTS + 1, B, K), F32),
            pltpu.VMEM((SLOTS + 1, B, K), F32),
            pltpu.VMEM((2, NZX, 4, ROWS, K), BF16),
            pltpu.VMEM((2, NZX, 4, ROWS, K), BF16),
            pltpu.VMEM((NZX, 4, ROWS, K), BF16),
            pltpu.VMEM((2, NZX, 4, ROWS, K), BF16),
            pltpu.VMEM((NROW, 4, COLS, K), BF16),
            pltpu.VMEM((2, NROW, 4, COLS, K), BF16),
            pltpu.SMEM((16,), jnp.int32),
            pltpu.SMEM((SLOTS, 2), jnp.int32),
            dma((SLOTS,)),
            dma((2, NZX)), dma((2, NZX)), dma((2, NZX)), dma((2, NZX)),
            dma((2, NROW)), dma((2, NROW)),
            dma((NZX,)), dma((NZX,)), dma((NZX,)), dma((NZX,)), dma((NROW,)), dma((NROW,)),
            dma((2,)), dma((2,)),
            dma((2, NZX)), dma((2, NZX)), dma((2, NROW)), dma((2, NROW)),
        ],
        name="swivel",
        compiler_params=pltpu.CompilerParams(
            collective_id=0, has_side_effects=True, vmem_limit_bytes=60 * 2**20
        ),
        cost_estimate=pl.CostEstimate(flops=6_400_000_000, bytes_accessed=9_000_000, transcendentals=8_000_000),
    )(tile_count.reshape(1), tile_list.reshape(SLOTS, 2), row_emb, col_emb, rowm, colm, tile_data)


def solution(mesh):
    placed = (
        P("row", "col", None),
        P("col", "row", None),
        P("row", "col"),
        P("col", "row"),
        P("row", "col", None, None),
        P("row", "col"),
        P("row", "col", None, None, None),
    )
    return jax.shard_map(
        shards,
        mesh=mesh,
        in_specs=placed,
        out_specs=(P("row", "col", None), P("col", "row", None)),
        check_vma=False,
    )
```

time: 704 us -> 117 us (0.17)
  waiting for transfers between devices: 563 us -> 0 us
  Pallas kernels: 0 us -> 108 us
  blocking collectives: 65.2 us -> 0 us
  matrix products: 18.6 us -> 0 us
  other arithmetic: 16.7 us -> 0 us
  between operations: 14.2 us -> 1.29 us
  loops' own time: 9.3 us -> 0 us
    reduce_scatter x4 -> x0, waiting for transfers between devices: 394 us -> none  [the longest x2 312 us: shards(): lax.psum_scatter(grad_rows.astype(jnp.bfloat16), 'col', scatter_dimension...]
    all_gather x4 -> x0, waiting for transfers between devices: 168 us -> none  [the longest x2 132 us: shards(): lax.all_gather(row_emb.astype(jnp.bfloat16), 'col', axis=1, tiled=True)]
    pallas_call x0 -> x1, Pallas kernels: none -> 108 us  [shards(): pl.pallas_call(kernel, out_shape=(jax.ShapeDtypeStruct(row_emb.shape, F32...]
    all_gather x2 -> x0, blocking collectives: 65.2 us -> none  [the longest x1 48.6 us: shards(): lax.all_gather(row_marg, 'col', axis=1, tiled=True)]
    dot_general x12 -> x0, matrix products: 18.6 us -> none  [the longest x4 9.03 us: one_tile(): lax.dot_general(row_piece, col_piece, (((1,), (1,)), ((), ())), preferred...]
    convert_element_type x9 -> x0, other arithmetic: 13.7 us -> none  [the longest x2 5.38 us: shards(): grad_rows.astype(jnp.bfloat16)]
    another operation x2 -> x0, loops' own time: 9.3 us -> none  [accumulate(): return lax.fori_loop(0, used_slots, one_tile, start)]
  transfers between devices with their start and end apart: 8 -> 0, of which waited for: 7 -> 0; matrix products, arithmetic and copies ran while one was open for 1% -> 0% of each run, Pallas kernels for 0% -> 0%
where the time goes in v1:
time: 117 us
  Pallas kernels  108 us (92%)
  local copies, waits for them, and re-layouts  7.22 us (6%)
  between operations  1.29 us (1%)
    pallas_call x1, Pallas kernels, shards(): pl.pallas_call(kernel, out_shape=(jax.ShapeDtypeStruct(row_emb.shape, F32...  108 us
    unnamed x2, local copies, waits for them, and re-layouts  3.15 us

profile of v1, /device:TPU:1, one launch (start us, length us, event | category | flops | bytes accessed | tf_op | source)
XLA Modules:
  0.0 116.9 jit_solution(11520727602262548975)
XLA Ops:
  1.3 0.8 reshape.16
  2.0 0.6 broadcast_in_dim.8.rowm_ref
  2.6 1.3 %copy.9.list_ref = s32[8,2]{1,0:T(8,128)} copy(s32[8,2]{0,1:T(2,128)} %bitcast.5) | data formatting | bytes 128 | tf_op jit(solution)/shard_map/reshape | solution.py:400
  4.0 0.7 tile.4
  4.7 0.7 tile.10.colm_ref
  5.4 108.4 %swivel.1 = (f32[4,16,256]{2,1,0:T(8,128)}, f32[4,64,256]{2,1,0:T(8,128)}) custom-call(s32[1]{0:T(128)} %bitcast.4.count_ref, s32[8,2]{1,0:T(8,128)} %copy.9.list_ref, f32[4,16,256]{2,1,0:T(8,128)} %row_ref.1, f32[4,64,256]{2,1,0:T(8,128)} %col_ref.1, bf16[16,128]{1,0:T(8,128)(2,1)} %broadcast_in_dim.8.rowm_ref, bf16[16,128]{1,0:T(8,128)(2,1)} %tile.10.colm_ref, ...), custom_call_target="tpu_custom_call" | custom-call | flops 6400000000 | bytes 9000000 | tf_op jit(solution)/shard_map/swivel/pallas_call | solution.py:360
  113.7 1.5 %copy.13 = f32[4,16,256]{2,1,0:T(8,128)} copy(f32[4,16,256]{2,1,0:T(8,128)} %get-tuple-element.4) | data formatting | bytes 131072
  115.2 1.7 %copy.14 = f32[4,64,256]{2,1,0:T(8,128)} copy(f32[4,64,256]{2,1,0:T(8,128)} %get-tuple-element.5) | data formatting | bytes 524288
  (1 shorter events, 0.0 us)

commit v2 on v0

v2 whole, which is shorter than its diff:
```python
import functools

import jax
import jax.numpy as jnp
from jax import lax
from jax.experimental import pallas as pl
from jax.experimental.pallas import tpu as pltpu
from jax.sharding import PartitionSpec as P

MESH = pl.DeviceIdType.MESH
BF16, F32 = jnp.bfloat16, jnp.float32
B, K = 512, 256
SLOTS = 8
NY = 4
NROW = 8
NZ = 8
NZX = 16
ROWS, COLS = 16, 64
NEAR = 5


def offset(n):
    odd = lax.rem(n, 2) if not isinstance(n, int) else n % 2
    return odd * ((n + 1) // 2) - (1 - odd) * (n // 2)


def kernel(
    count_ref, list_ref, row_ref, col_ref, rowm_ref, colm_ref, data_ref, row_out, col_out,
    row_got_panel, col_panel, row_panel, tile_f32, picked, marg_left, marg_right, bias, weight,
    stage, row_term, col_term, row_send, row_half, row_sum, row_far, row_last, row_got,
    col_send, col_cross, col_got, slot_of, pair_of,
    data_sem, rp_s, rp_r, rf_s, rf_r, cp_s, cp_r,
    sib_s, sib_r, rg_s, rg_r, cg_s, cg_r,
):
    r, c = lax.axis_index("row"), lax.axis_index("col")
    xl, y = r // NY, lax.rem(r, NY)
    zx, core = c // 2, lax.rem(c, 2)
    z, xh = zx // 2, lax.rem(zx, 2)
    sibling = {"row": r, "col": zx * 2 + (1 - core)}
    across = (1 - xl) * NY + y

    def at_z(dz, other=0):
        side = xh if other == 0 else 1 - xh
        return {"row": r, "col": (lax.rem(z + dz + NZ, NZ) * 2 + side) * 2 + core}

    def at_y(dy):
        return {"row": xl * NY + lax.rem(y + dy, NY), "col": c}

    def at_x():
        return {"row": across, "col": c}

    def copy(src, dst, send, recv, device):
        return pltpu.make_async_remote_copy(
            src_ref=src, dst_ref=dst, send_sem=send, recv_sem=recv, device_id=device, device_id_type=MESH
        )

    def loop(lo, hi, body):
        def step(i, carry):
            body(i)
            return carry

        lax.fori_loop(lo, hi, step, 0)

    barrier = pltpu.get_barrier_semaphore()
    partners = [at_z(dz, other) for dz in (2, -2, 1, -1) for other in (0, 1)] + [at_z(0, 1)]
    partners += [at_y(dy) for dy in (2, 1, 3)] + [at_x(), sibling]
    for device in partners:
        pl.semaphore_signal(barrier, inc=1, device_id=device, device_id_type=MESH)

    def data_copy(s):
        return pltpu.make_async_copy(data_ref.at[0, 0, s], stage.at[s], data_sem.at[s])

    loop(0, SLOTS, lambda s: data_copy(s).start())

    row_out[...] = row_ref[...]
    col_out[...] = col_ref[...]
    tile_f32[...] = jnp.zeros((2, 16, K), F32)
    tile_f32[0, 0:4, 0:ROWS] = rowm_ref[...].astype(F32)
    tile_f32[1, 0:4, 0:COLS] = colm_ref[...].astype(F32)
    row_got_panel[0, core, 0, xh, 4] = tile_f32[0].astype(BF16)
    col_panel[0, r, 16] = tile_f32[1].astype(BF16)

    def pieces(p):
        return pl.ds(0, 5 if p == 0 else 4)

    def col_rows(p):
        return pl.ds(0, 17 if p == 0 else 16)

    def row_direct(p):
        mine = row_got_panel.at[p, core, 0, xh, pieces(p)]
        out = []
        for n in (3, 4, 1, 2, 0):
            for other in (0, 1):
                if n == 0 and other == 0:
                    continue
                sem = n * 2 + other
                there = row_got_panel.at[p, core, n, xh, pieces(p)]
                side = xh if other == 0 else 1 - xh
                here = row_got_panel.at[p, core, n, side, pieces(p)]
                device = at_z(offset(n), other)
                send = functools.partial(copy, mine, there, rp_s.at[p, sem], rp_r.at[p, sem], device)
                recv = functools.partial(copy, here, here, rp_s.at[p, sem], rp_r.at[p, sem], device)
                out.append((n, send, recv))
        return out

    def row_relay(p):
        out = []
        for sem, (src, dst, dz, side) in enumerate([(3, 5, 1, None), (4, 6, -1, None), (3, 7, 2, 0), (4, 7, -2, 1)]):
            at = pl.ds(0, 2) if side is None else pl.ds(side, 1)
            here = row_got_panel.at[p, core, src, at, pieces(p)]
            there = row_got_panel.at[p, core, dst, at, pieces(p)]
            out.append(copy(here, there, rp_s.at[p, 10 + sem], rp_r.at[p, 10 + sem], at_z(dz)))
        return out

    def row_hand(p, part, side):
        slots = pl.ds(0, NEAR) if part == 0 else pl.ds(NEAR, 8 - NEAR)
        block = row_got_panel.at[p, side, slots, :, pieces(p)]
        return copy(block, block, rf_s.at[p, part], rf_r.at[p, part], sibling)

    def col_direct(p, q):
        mine = col_panel.at[p, r, col_rows(p)]
        device = at_x() if q == NY else at_y(q)
        return copy(mine, mine, cp_s.at[p, q], cp_r.at[p, q], device)

    def col_direct_got(p, q):
        source = across if q == NY else xl * NY + lax.rem(y - q + NY, NY)
        got = col_panel.at[p, source, col_rows(p)]
        return copy(got, got, cp_s.at[p, q], cp_r.at[p, q], at_x())

    def col_pass(p, q):
        got = col_panel.at[p, across, col_rows(p)]
        return copy(got, got, cp_s.at[p, NY + q], cp_r.at[p, NY + q], at_y(q))

    def col_pass_got(p, q):
        source = (1 - xl) * NY + lax.rem(y - q + NY, NY)
        got = col_panel.at[p, source, col_rows(p)]
        return copy(got, got, cp_s.at[p, NY + q], cp_r.at[p, NY + q], at_x())

    ys = (2, 1, 3)

    def col_gather_send(p):
        for j in range(4):
            col_panel[p, r, 4 * j : 4 * j + 4] = col_out[j].astype(BF16).reshape(4, 16, K)
        col_direct(p, NY).start()
        for q in ys:
            col_direct(p, q).start()

    def row_gather_send(p):
        row_got_panel[p, core, 0, xh, 0:4] = row_out[...].astype(BF16)
        for _, send, _ in row_direct(p):
            send().start()

    def pass_on(p):
        col_direct_got(p, NY).wait_recv()
        for q in ys:
            col_pass(p, q).start()

    def relay(p):
        for n, _, recv in row_direct(p):
            if n in (3, 4):
                recv().wait_recv()
        for send in row_relay(p):
            send.start()

    def hand_near(p):
        for n, _, recv in row_direct(p):
            if n not in (3, 4):
                recv().wait_recv()
        row_hand(p, 0, core).start()

    def hand_far(p):
        for send in row_relay(p):
            send.wait_recv()
        row_hand(p, 1, core).start()

    def gather_end(p):
        for q in ys:
            col_direct_got(p, q).wait_recv()
        for q in ys:
            col_pass_got(p, q).wait_recv()
        for part in range(2):
            row_hand(p, part, 1 - core).wait_recv()

    def gather_sent(p):
        for _, send, _ in row_direct(p):
            send().wait_send()
        for send in row_relay(p):
            send.wait_send()
        for part in range(2):
            row_hand(p, part, core).wait_send()
        for q in (NY,) + ys:
            col_direct(p, q).wait_send()
        for q in ys:
            col_pass(p, q).wait_send()

    def arrange(p):
        def slot(n):
            source = lax.rem(z - offset(n) + 2 * NZ, NZ)
            for side in range(2):
                for k in range(2):
                    rows = pl.ds(pl.multiple_of(source * 64 + side * 32 + k * ROWS, ROWS), ROWS)
                    for i in range(4):
                        row_panel[i, rows, :] = row_got_panel[p, k, n, side, i]

        loop(0, 8, slot)

    pl.semaphore_wait(barrier, len(partners))
    col_gather_send(0)
    row_gather_send(0)

    row_term[SLOTS] = jnp.zeros((B, K), F32)
    col_term[SLOTS] = jnp.zeros((B, K), F32)
    codes = []
    for s in range(SLOTS):
        i = jnp.clip(list_ref[0, s] - r * 4, 0, 3)
        j = jnp.clip(list_ref[1, s] - c * 4, 0, 3)
        pair_of[s, 0] = i
        pair_of[s, 1] = j
        codes.append(jnp.where(s < count_ref[0, 0], i * 4 + j, -1))
    for pair in range(16):
        found = jnp.int32(SLOTS)
        for s in range(SLOTS):
            found = jnp.where(codes[s] == pair, s, found)
        slot_of[pair] = found

    def prepare(s):
        data_copy(s).wait()

        def part(h, carry):
            rows = pl.ds(pl.multiple_of(h * 64, 64), 64)
            level = stage[s, rows].astype(F32)
            bias[s, rows] = -jnp.log(jnp.maximum(level, 1.0)).astype(BF16)
            weight[s, rows] = jnp.where(level > 0.0, 0.1 + 0.25 * jnp.sqrt(level), 0.0).astype(BF16)
            return carry

        lax.fori_loop(0, B // 64, part, 0)

    loop(0, 4, prepare)
    pass_on(0)
    loop(4, 6, prepare)
    relay(0)
    hand_near(0)
    loop(6, SLOTS, prepare)
    hand_far(0)
    gather_end(0)
    arrange(0)

    lane = lax.broadcasted_iota(jnp.int32, (ROWS, 128), 1)
    mine = lane == lax.broadcasted_iota(jnp.int32, (ROWS, 128), 0)

    def pick(n):
        source = lax.rem(z - offset(n) + 2 * NZ, NZ)
        for side in range(2):
            for k in range(2):
                rows = pl.ds(pl.multiple_of(source * 64 + side * 32 + k * ROWS, ROWS), ROWS)
                margins = row_got_panel[0, k, n, side, 4].astype(F32)
                for i in range(4):
                    line = jnp.broadcast_to(margins[i : i + 1, 0:128], (ROWS, 128))
                    picked[i, rows, :] = jnp.where(mine, line, 0.0).astype(BF16)

    loop(0, 8, pick)
    ones = jnp.ones((128, 128), BF16)
    for i in range(4):
        marg_left[i] = jnp.dot(picked[i], ones, preferred_element_type=F32)
    for g in range(NROW // 2):
        low = col_panel[0, 2 * g, 16].astype(F32)[:, 0:128]
        high = col_panel[0, 2 * g + 1, 16].astype(F32)[:, 0:128]
        marg_right[:, g * 128 : (g + 1) * 128] = jnp.where(lane < COLS, low, pltpu.roll(high, COLS, 1))

    def tiles(p):
        def tile(s):
            i, j = pair_of[s, 0], pair_of[s, 1]
            col_piece = col_panel[p, :, pl.ds(4 * j, 4)].reshape(B, K)
            row_piece = row_panel[i]
            scores = lax.dot_general(row_piece, col_piece, (((1,), (1,)), ((), ())), preferred_element_type=F32)
            if p == 0:
                left = jnp.concatenate([marg_left[i]] * (B // 128), axis=1)
                shift = (bias[s].astype(F32) + marg_right[pl.ds(j, 1), :] + left).astype(BF16)
                bias[s] = shift
            else:
                shift = bias[s]
            diff = scores.astype(BF16) + shift
            scale = weight[s]
            signal = jnp.where(scale > 0, scale * diff, 0.5 * jnp.tanh(0.5 * diff) + 0.5).astype(BF16)
            row_term[s] = jnp.dot(signal, col_piece, preferred_element_type=F32)
            col_term[s] = lax.dot_general(signal, row_piece, (((0,), (0,)), ((), ())), preferred_element_type=F32)

        loop(0, SLOTS, tile)

    far, near = pl.ds(NEAR, 8 - NEAR), pl.ds(0, NEAR)

    def sibling_send(p, part):
        slots = near if part == 0 else far
        return copy(
            row_send.at[1 - core, slots], row_half.at[p, slots], sib_s.at[p, part], sib_r.at[p, part], sibling
        )

    def far_sends(p):
        return [
            copy(row_sum.at[5], row_far.at[p, 0], rg_s.at[p, 10], rg_r.at[p, 10], at_z(1)),
            copy(row_sum.at[6], row_far.at[p, 1], rg_s.at[p, 11], rg_r.at[p, 11], at_z(-1)),
            copy(row_sum.at[7, 0], row_last.at[p, 0], rg_s.at[p, 12], rg_r.at[p, 12], at_z(2)),
            copy(row_sum.at[7, 1], row_last.at[p, 1], rg_s.at[p, 13], rg_r.at[p, 13], at_z(-2)),
        ]

    def near_sends(p, slots):
        out = []
        for m in slots:
            for other in (0, 1):
                if m == 0 and other == 0:
                    continue
                sem = m * 2 + other
                side = xh if other == 0 else 1 - xh
                out.append(
                    copy(
                        row_sum.at[m, side], row_got.at[p, sem], rg_s.at[p, sem], rg_r.at[p, sem],
                        at_z(offset(m), other),
                    )
                )
        return out

    def cross_send(p, q):
        t = (1 - xl) * NY + lax.rem(y + q, NY)
        return copy(col_send.at[t], col_cross.at[p, q], cg_s.at[p, NY + q], cg_r.at[p, NY + q], at_y(q))

    def straight_send(p, q):
        t = xl * NY + lax.rem(y + q, NY)
        return copy(col_send.at[t], col_got.at[p, q], cg_s.at[p, q], cg_r.at[p, q], at_y(q))

    def across_send(p):
        return copy(col_send.at[across], col_got.at[p, 0], cg_s.at[p, NY], cg_r.at[p, NY], at_x())

    def row_part(m):
        dest = lax.rem(z + offset(m) + NZ, NZ)
        for side in range(2):
            for k in range(2):
                rows = pl.ds(pl.multiple_of(dest * 64 + side * 32 + k * ROWS, ROWS), ROWS)
                for i in range(4):
                    found = [row_term[slot_of[i * 4 + j], rows, :] for j in range(4)]
                    row_send[k, m, side, i] = ((found[0] + found[1]) + (found[2] + found[3])).astype(BF16)

    def col_part(t):
        for part in range(2):
            rows = pl.ds(pl.multiple_of(t * COLS + part * 32, 32), 32)
            for j in range(4):
                found = [col_term[slot_of[i * 4 + j], rows, :] for i in range(4)]
                col_send[t, j, part * 32 : part * 32 + 32] = (
                    (found[0] + found[1]) + (found[2] + found[3])
                ).astype(BF16)

    def add(p, m):
        for side in range(2):
            row_sum[m, side] = (
                row_send[core, m, side].astype(F32) + row_half[p, m, side].astype(F32)
            ).astype(BF16)

    def scatter(p):
        loop(NEAR, 8, row_part)
        sibling_send(p, 1).start()
        loop(0, NEAR, row_part)
        sibling_send(p, 0).start()
        loop(0, NY, lambda t: col_part((1 - xl) * NY + t))
        for q in ys:
            cross_send(p, q).start()
        sibling_send(p, 1).wait_recv()
        for m in range(NEAR, 8):
            add(p, m)
        for send in far_sends(p):
            send.start()
        loop(0, NY, lambda t: col_part(xl * NY + t))
        for q in ys:
            straight_send(p, q).start()
        sibling_send(p, 0).wait_recv()
        for m in range(NEAR):
            add(p, m)
        for send in near_sends(p, (1, 2, 0)):
            send.start()
        for send in far_sends(p):
            send.wait_recv()
        for m, e in ((3, 0), (4, 1)):
            for side in range(2):
                total = row_sum[m, side].astype(F32) + row_far[p, e, side].astype(F32)
                if side == e:
                    total = total + row_last[p, e].astype(F32)
                row_sum[m, side] = total.astype(BF16)
        for send in near_sends(p, (3, 4)):
            send.start()
        for q in ys:
            cross_send(p, q).wait_recv()
        for j in range(4):
            total = col_send[across, j].astype(F32)
            for q in ys:
                total = total + col_cross[p, q, j].astype(F32)
            col_send[across, j] = total.astype(BF16)
        across_send(p).start()

    def row_update(p):
        for send in near_sends(p, range(NEAR)):
            send.wait_recv()
        total = row_sum[0, xh].astype(F32)
        for sem in range(1, 2 * NEAR):
            total = total + row_got[p, sem].astype(F32)
        row_out[...] = row_out[...] - 0.0004 * total

    def col_update(p):
        for q in ys:
            straight_send(p, q).wait_recv()
        across_send(p).wait_recv()
        for j in range(4):
            total = col_send[r, j].astype(F32)
            for q in range(NY):
                total = total + col_got[p, q, j].astype(F32)
            col_out[j] = col_out[j] - 0.0004 * total

    def scatter_sent(p):
        for q in ys:
            cross_send(p, q).wait_send()
            straight_send(p, q).wait_send()
        across_send(p).wait_send()
        for send in far_sends(p) + near_sends(p, range(NEAR)):
            send.wait_send()
        for part in range(2):
            sibling_send(p, part).wait_send()

    tiles(0)
    scatter(0)
    row_update(0)
    row_gather_send(1)
    col_update(0)
    col_gather_send(1)
    scatter_sent(0)
    pass_on(1)
    relay(1)
    hand_near(1)
    hand_far(1)
    gather_end(1)
    arrange(1)
    tiles(1)
    scatter(1)
    row_update(1)
    col_update(1)
    scatter_sent(1)
    gather_sent(0)
    gather_sent(1)


def shards(row_emb, col_emb, row_marg, col_marg, tile_list, tile_count, tile_data):
    vmem = pl.BlockSpec(memory_space=pltpu.VMEM)
    smem = pl.BlockSpec(memory_space=pltpu.SMEM)
    dma = pltpu.SemaphoreType.DMA
    return pl.pallas_call(
        kernel,
        out_shape=(
            jax.ShapeDtypeStruct(row_emb.shape, F32),
            jax.ShapeDtypeStruct(col_emb.shape, F32),
        ),
        in_specs=[smem, smem, vmem, vmem, vmem, vmem, pl.BlockSpec(memory_space=pl.ANY)],
        out_specs=(vmem, vmem),
        scratch_shapes=[
            pltpu.VMEM((2, 2, 8, 2, 5, ROWS, K), BF16),
            pltpu.VMEM((2, NROW, 17, 16, K), BF16),
            pltpu.VMEM((4, B, K), BF16),
            pltpu.VMEM((2, 16, K), F32),
            pltpu.VMEM((4, B, 128), BF16),
            pltpu.VMEM((4, B, 128), F32),
            pltpu.VMEM((16, B), F32),
            pltpu.VMEM((SLOTS, B, B), BF16),
            pltpu.VMEM((SLOTS, B, B), BF16),
            pltpu.VMEM((SLOTS, B, B), jnp.int32),
            pltpu.VMEM((SLOTS + 1, B, K), F32),
            pltpu.VMEM((SLOTS + 1, B, K), F32),
            pltpu.VMEM((2, 8, 2, 4, ROWS, K), BF16),
            pltpu.VMEM((2, 8, 2, 4, ROWS, K), BF16),
            pltpu.VMEM((8, 2, 4, ROWS, K), BF16),
            pltpu.VMEM((2, 2, 2, 4, ROWS, K), BF16),
            pltpu.VMEM((2, 2, 4, ROWS, K), BF16),
            pltpu.VMEM((2, 2 * NEAR, 4, ROWS, K), BF16),
            pltpu.VMEM((NROW, 4, COLS, K), BF16),
            pltpu.VMEM((2, NY, 4, COLS, K), BF16),
            pltpu.VMEM((2, NY, 4, COLS, K), BF16),
            pltpu.SMEM((16,), jnp.int32),
            pltpu.SMEM((SLOTS, 2), jnp.int32),
            dma((SLOTS,)),
            dma((2, 14)), dma((2, 14)), dma((2, 2)), dma((2, 2)), dma((2, NROW)), dma((2, NROW)),
            dma((2, 2)), dma((2, 2)), dma((2, 14)), dma((2, 14)), dma((2, NROW)), dma((2, NROW)),
        ],
        name="swivel",
        compiler_params=pltpu.CompilerParams(
            collective_id=0, has_side_effects=True, vmem_limit_bytes=60 * 2**20
        ),
        cost_estimate=pl.CostEstimate(flops=6_400_000_000, bytes_accessed=9_000_000, transcendentals=8_000_000),
    )(tile_count, tile_list[0, 0].T, row_emb, col_emb, row_marg, col_marg, tile_data)


def solution(mesh):
    placed = (
        P("row", "col", None),
        P("col", "row", None),
        P("row", "col"),
        P("col", "row"),
        P("row", "col", None, None),
        P("row", "col"),
        P("row", "col", None, None, None),
    )
    return jax.shard_map(
        shards,
        mesh=mesh,
        in_specs=placed,
        out_specs=(P("row", "col", None), P("col", "row", None)),
        check_vma=False,
    )
```

time: 704 us -> 90.9 us (0.13)
  waiting for transfers between devices: 563 us -> 0 us
  Pallas kernels: 0 us -> 86.3 us
  blocking collectives: 65.2 us -> 0 us
  matrix products: 18.6 us -> 0 us
  other arithmetic: 16.7 us -> 0 us
  between operations: 14.2 us -> 1.29 us
  loops' own time: 9.3 us -> 0 us
  local copies, waits for them, and re-layouts: 10.6 us -> 3.15 us
    reduce_scatter x4 -> x0, waiting for transfers between devices: 394 us -> none  [the longest x2 312 us: shards(): lax.psum_scatter(grad_rows.astype(jnp.bfloat16), 'col', scatter_dimension...]
    all_gather x4 -> x0, waiting for transfers between devices: 168 us -> none  [the longest x2 132 us: shards(): lax.all_gather(row_emb.astype(jnp.bfloat16), 'col', axis=1, tiled=True)]
    pallas_call x0 -> x1, Pallas kernels: none -> 86.3 us  [shards(): pl.pallas_call(kernel, out_shape=(jax.ShapeDtypeStruct(row_emb.shape, F32...]
    all_gather x2 -> x0, blocking collectives: 65.2 us -> none  [the longest x1 48.6 us: shards(): lax.all_gather(row_marg, 'col', axis=1, tiled=True)]
    dot_general x12 -> x0, matrix products: 18.6 us -> none  [the longest x4 9.03 us: one_tile(): lax.dot_general(row_piece, col_piece, (((1,), (1,)), ((), ())), preferred...]
    convert_element_type x9 -> x0, other arithmetic: 13.7 us -> none  [the longest x2 5.38 us: shards(): grad_rows.astype(jnp.bfloat16)]
    another operation x2 -> x0, loops' own time: 9.3 us -> none  [accumulate(): return lax.fori_loop(0, used_slots, one_tile, start)]
  transfers between devices with their start and end apart: 8 -> 0, of which waited for: 7 -> 0; matrix products, arithmetic and copies ran while one was open for 1% -> 0% of each run, Pallas kernels for 0% -> 0%
where the time goes in v2:
time: 90.9 us; the launch traced here: 90.7 us
  Pallas kernels  86.3 us (95%)
  local copies, waits for them, and re-layouts  3.15 us (3%)
  between operations  1.29 us (1%)
    pallas_call x1, Pallas kernels, shards(): pl.pallas_call(kernel, out_shape=(jax.ShapeDtypeStruct(row_emb.shape, F32...  86.3 us
    unnamed x2, local copies, waits for them, and re-layouts  3.15 us

profile of v2, /device:TPU:1, one launch (start us, length us, event | category | flops | bytes accessed | tf_op | source)
XLA Modules:
  0.0 90.7 jit_solution(2766988958234172535)
XLA Ops:
  1.3 86.3 %swivel.1 = (f32[4,16,256]{2,1,0:T(8,128)}, f32[4,64,256]{2,1,0:T(8,128)}) custom-call(s32[1,1]{1,0:T(1,128)S(6)} %copy.11.count_ref, s32[2,8]{1,0:T(2,128)} %bitcast.3, f32[4,16,256]{2,1,0:T(8,128)} %row_ref.1, f32[4,64,256]{2,1,0:T(8,128)} %col_ref.1, bf16[4,16]{1,0:T(4,128)(2,1)} %rowm_ref.1, bf16[4,64]{1,0:T(4,128)(2,1)} %colm_ref.1, ...), custom_call_target="tpu_custom_call" | custom-call | flops 6400000000 | bytes 9000000 | tf_op jit(solution)/shard_map/swivel/pallas_call | solution.py:451
  87.6 1.5 %copy.12 = f32[4,16,256]{2,1,0:T(8,128)} copy(f32[4,16,256]{2,1,0:T(8,128)} %get-tuple-element.4) | data formatting | bytes 131072
  89.0 1.7 %copy.13 = f32[4,64,256]{2,1,0:T(8,128)} copy(f32[4,64,256]{2,1,0:T(8,128)} %get-tuple-element.5) | data formatting | bytes 524288

commit v3 on v2

--- a/solution.py
+++ b/solution.py
@@ -25,11 +25,11 @@
 
 
 def kernel(
-    count_ref, list_ref, row_ref, col_ref, rowm_ref, colm_ref, data_ref, row_out, col_out,
+    count_ref, list_ref, row_ref, col_ref, rowm_ref, colm_ref, data_ref, row_out, col_out, row_now, col_now,
     row_got_panel, col_panel, row_panel, tile_f32, picked, marg_left, marg_right, bias, weight,
     stage, row_term, col_term, row_send, row_half, row_sum, row_far, row_last, row_got,
     col_send, col_cross, col_got, slot_of, pair_of,
-    data_sem, rp_s, rp_r, rf_s, rf_r, cp_s, cp_r,
+    data_sem, in_sem, out_sem, rp_s, rp_r, rf_s, rf_r, cp_s, cp_r,
     sib_s, sib_r, rg_s, rg_r, cg_s, cg_r,
 ):
     r, c = lax.axis_index("row"), lax.axis_index("col")
@@ -70,15 +70,19 @@
     def data_copy(s):
         return pltpu.make_async_copy(data_ref.at[0, 0, s], stage.at[s], data_sem.at[s])
 
+    row_in = pltpu.make_async_copy(row_ref, row_now, in_sem.at[0])
+    col_in = pltpu.make_async_copy(col_ref, col_now, in_sem.at[1])
+    row_in.start()
+    col_in.start()
     loop(0, SLOTS, lambda s: data_copy(s).start())
 
-    row_out[...] = row_ref[...]
-    col_out[...] = col_ref[...]
     tile_f32[...] = jnp.zeros((2, 16, K), F32)
     tile_f32[0, 0:4, 0:ROWS] = rowm_ref[...].astype(F32)
     tile_f32[1, 0:4, 0:COLS] = colm_ref[...].astype(F32)
     row_got_panel[0, core, 0, xh, 4] = tile_f32[0].astype(BF16)
     col_panel[0, r, 16] = tile_f32[1].astype(BF16)
+    row_in.wait()
+    col_in.wait()
 
     def pieces(p):
         return pl.ds(0, 5 if p == 0 else 4)
@@ -128,8 +132,9 @@
         return copy(got, got, cp_s.at[p, q], cp_r.at[p, q], at_x())
 
     def col_pass(p, q):
-        got = col_panel.at[p, across, col_rows(p)]
-        return copy(got, got, cp_s.at[p, NY + q], cp_r.at[p, NY + q], at_y(q))
+        source = xl * NY + lax.rem(y + 2, NY) if q == 2 else across
+        got = col_panel.at[p, source, col_rows(p)]
+        return copy(got, got, cp_s.at[p, NY + q], cp_r.at[p, NY + q], at_x() if q == 2 else at_y(q))
 
     def col_pass_got(p, q):
         source = (1 - xl) * NY + lax.rem(y - q + NY, NY)
@@ -139,21 +144,29 @@
     ys = (2, 1, 3)
 
     def col_gather_send(p):
-        for j in range(4):
-            col_panel[p, r, 4 * j : 4 * j + 4] = col_out[j].astype(BF16).reshape(4, 16, K)
         col_direct(p, NY).start()
         for q in ys:
             col_direct(p, q).start()
 
+    def col_round(p):
+        for j in range(4):
+            col_panel[p, r, 4 * j : 4 * j + 4] = col_now[j].astype(BF16).reshape(4, 16, K)
+
+    def row_round(p):
+        row_got_panel[p, core, 0, xh, 0:4] = row_now[...].astype(BF16)
+
     def row_gather_send(p):
-        row_got_panel[p, core, 0, xh, 0:4] = row_out[...].astype(BF16)
         for _, send, _ in row_direct(p):
             send().start()
 
     def pass_on(p):
         col_direct_got(p, NY).wait_recv()
-        for q in ys:
+        for q in (1, 3):
             col_pass(p, q).start()
+
+    def pass_back(p):
+        col_direct_got(p, 2).wait_recv()
+        col_pass(p, 2).start()
 
     def relay(p):
         for n, _, recv in row_direct(p):
@@ -174,7 +187,7 @@
         row_hand(p, 1, core).start()
 
     def gather_end(p):
-        for q in ys:
+        for q in (1, 3):
             col_direct_got(p, q).wait_recv()
         for q in ys:
             col_pass_got(p, q).wait_recv()
@@ -204,6 +217,8 @@
 
         loop(0, 8, slot)
 
+    col_round(0)
+    row_round(0)
     pl.semaphore_wait(barrier, len(partners))
     col_gather_send(0)
     row_gather_send(0)
@@ -237,7 +252,9 @@
 
     loop(0, 4, prepare)
     pass_on(0)
-    loop(4, 6, prepare)
+    prepare(4)
+    pass_back(0)
+    prepare(5)
     relay(0)
     hand_near(0)
     loop(6, SLOTS, prepare)
@@ -285,7 +302,8 @@
             row_term[s] = jnp.dot(signal, col_piece, preferred_element_type=F32)
             col_term[s] = lax.dot_general(signal, row_piece, (((0,), (0,)), ((), ())), preferred_element_type=F32)
 
-        loop(0, SLOTS, tile)
+        for s in range(SLOTS):
+            tile(s)
 
     far, near = pl.ds(NEAR, 8 - NEAR), pl.ds(0, NEAR)
 
@@ -321,7 +339,8 @@
 
     def cross_send(p, q):
         t = (1 - xl) * NY + lax.rem(y + q, NY)
-        return copy(col_send.at[t], col_cross.at[p, q], cg_s.at[p, NY + q], cg_r.at[p, NY + q], at_y(q))
+        device = at_x() if q == 2 else at_y(q)
+        return copy(col_send.at[t], col_cross.at[p, q], cg_s.at[p, NY + q], cg_r.at[p, NY + q], device)
 
     def straight_send(p, q):
         t = xl * NY + lax.rem(y + q, NY)
@@ -354,27 +373,46 @@
                 row_send[core, m, side].astype(F32) + row_half[p, m, side].astype(F32)
             ).astype(BF16)
 
+    def col_add(p, t, crossed):
+        for j in range(4):
+            total = col_send[t, j].astype(F32)
+            for q in crossed:
+                total = total + col_cross[p, q, j].astype(F32)
+            col_send[t, j] = total.astype(BF16)
+
     def scatter(p):
         loop(NEAR, 8, row_part)
         sibling_send(p, 1).start()
+        col_part((1 - xl) * NY + lax.rem(y + 2, NY))
+        cross_send(p, 2).start()
         loop(0, NEAR, row_part)
         sibling_send(p, 0).start()
-        loop(0, NY, lambda t: col_part((1 - xl) * NY + t))
-        for q in ys:
+        for q in (1, 3):
+            col_part((1 - xl) * NY + lax.rem(y + q, NY))
             cross_send(p, q).start()
         sibling_send(p, 1).wait_recv()
         for m in range(NEAR, 8):
             add(p, m)
         for send in far_sends(p):
             send.start()
-        loop(0, NY, lambda t: col_part(xl * NY + t))
-        for q in ys:
-            straight_send(p, q).start()
+        col_part(xl * NY + lax.rem(y + 2, NY))
+        col_part(across)
         sibling_send(p, 0).wait_recv()
         for m in range(NEAR):
             add(p, m)
         for send in near_sends(p, (1, 2, 0)):
             send.start()
+        for q in (1, 3):
+            col_part(xl * NY + lax.rem(y + q, NY))
+            straight_send(p, q).start()
+        col_part(r)
+        cross_send(p, 2).wait_recv()
+        col_add(p, xl * NY + lax.rem(y + 2, NY), (2,))
+        straight_send(p, 2).start()
+        for q in (1, 3):
+            cross_send(p, q).wait_recv()
+        col_add(p, across, (1, 3))
+        across_send(p).start()
         for send in far_sends(p):
             send.wait_recv()
         for m, e in ((3, 0), (4, 1)):
@@ -385,14 +423,6 @@
                 row_sum[m, side] = total.astype(BF16)
         for send in near_sends(p, (3, 4)):
             send.start()
-        for q in ys:
-            cross_send(p, q).wait_recv()
-        for j in range(4):
-            total = col_send[across, j].astype(F32)
-            for q in ys:
-                total = total + col_cross[p, q, j].astype(F32)
-            col_send[across, j] = total.astype(BF16)
-        across_send(p).start()
 
     def row_update(p):
         for send in near_sends(p, range(NEAR)):
@@ -400,7 +430,7 @@
         total = row_sum[0, xh].astype(F32)
         for sem in range(1, 2 * NEAR):
             total = total + row_got[p, sem].astype(F32)
-        row_out[...] = row_out[...] - 0.0004 * total
+        row_now[...] = row_now[...] - 0.0004 * total
 
     def col_update(p):
         for q in ys:
@@ -410,7 +440,7 @@
             total = col_send[r, j].astype(F32)
             for q in range(NY):
                 total = total + col_got[p, q, j].astype(F32)
-            col_out[j] = col_out[j] - 0.0004 * total
+            col_now[j] = col_now[j] - 0.0004 * total
 
     def scatter_sent(p):
         for q in ys:
@@ -425,11 +455,14 @@
     tiles(0)
     scatter(0)
     row_update(0)
+    row_round(1)
     row_gather_send(1)
     col_update(0)
+    col_round(1)
     col_gather_send(1)
     scatter_sent(0)
     pass_on(1)
+    pass_back(1)
     relay(1)
     hand_near(1)
     hand_far(1)
@@ -438,25 +471,47 @@
     tiles(1)
     scatter(1)
     row_update(1)
+    row_back = pltpu.make_async_copy(row_now, row_out, out_sem.at[0])
+    row_back.start()
     col_update(1)
+    col_back = pltpu.make_async_copy(col_now, col_out, out_sem.at[1])
+    col_back.start()
     scatter_sent(1)
     gather_sent(0)
     gather_sent(1)
+    row_back.wait()
+    col_back.wait()
+
+
+def finish(row_ref, col_ref, row_out, col_out, row_now, col_now, sem):
+    ways = [(row_ref, row_now, row_out), (col_ref, col_now, col_out)]
+    coming = [pltpu.make_async_copy(src, now, sem.at[k]) for k, (src, now, _) in enumerate(ways)]
+    going = [pltpu.make_async_copy(now, dst, sem.at[2 + k]) for k, (_, now, dst) in enumerate(ways)]
+    for copy in coming:
+        copy.start()
+    for k in range(2):
+        coming[k].wait()
+        going[k].start()
+    for copy in going:
+        copy.wait()
 
 
 def shards(row_emb, col_emb, row_marg, col_marg, tile_list, tile_count, tile_data):
     vmem = pl.BlockSpec(memory_space=pltpu.VMEM)
     smem = pl.BlockSpec(memory_space=pltpu.SMEM)
     dma = pltpu.SemaphoreType.DMA
-    return pl.pallas_call(
+    where = pl.BlockSpec(memory_space=pl.ANY)
+    news = pl.pallas_call(
         kernel,
         out_shape=(
             jax.ShapeDtypeStruct(row_emb.shape, F32),
             jax.ShapeDtypeStruct(col_emb.shape, F32),
         ),
-        in_specs=[smem, smem, vmem, vmem, vmem, vmem, pl.BlockSpec(memory_space=pl.ANY)],
-        out_specs=(vmem, vmem),
+        in_specs=[smem, smem, where, where, vmem, vmem, where],
+        out_specs=(where, where),
         scratch_shapes=[
+            pltpu.VMEM(row_emb.shape, F32),
+            pltpu.VMEM(col_emb.shape, F32),
             pltpu.VMEM((2, 2, 8, 2, 5, ROWS, K), BF16),
             pltpu.VMEM((2, NROW, 17, 16, K), BF16),
             pltpu.VMEM((4, B, K), BF16),
@@ -480,7 +535,7 @@
             pltpu.VMEM((2, NY, 4, COLS, K), BF16),
             pltpu.SMEM((16,), jnp.int32),
             pltpu.SMEM((SLOTS, 2), jnp.int32),
-            dma((SLOTS,)),
+            dma((SLOTS,)), dma((2,)), dma((2,)),
             dma((2, 14)), dma((2, 14)), dma((2, 2)), dma((2, 2)), dma((2, NROW)), dma((2, NROW)),
             dma((2, 2)), dma((2, 2)), dma((2, 14)), dma((2, 14)), dma((2, NROW)), dma((2, NROW)),
         ],
@@ -490,6 +545,14 @@
         ),
         cost_estimate=pl.CostEstimate(flops=6_400_000_000, bytes_accessed=9_000_000, transcendentals=8_000_000),
     )(tile_count, tile_list[0, 0].T, row_emb, col_emb, row_marg, col_marg, tile_data)
+    return pl.pallas_call(
+        finish,
+        out_shape=tuple(jax.ShapeDtypeStruct(new.shape, F32) for new in news),
+        in_specs=[where, where],
+        out_specs=(where, where),
+        scratch_shapes=[pltpu.VMEM(new.shape, F32) for new in news] + [dma((4,))],
+        name="finish",
+    )(*news)
 
 
 def solution(mesh):

time: 90.9 us -> 82.4 us (0.906)
  the two profiles are of different devices: /device:TPU:1 before, /device:TPU:32 now
where the time goes in v3:
time: 82.4 us; the launch traced here: 82.2 us
  Pallas kernels  81 us (98%)
  between operations  1.29 us (2%)
    pallas_call x1, Pallas kernels, shards(): pl.pallas_call(kernel, out_shape=(jax.ShapeDtypeStruct(row_emb.shape, F32...  79.2 us
    pallas_call x1, Pallas kernels, shards(): pl.pallas_call(finish, out_shape=tuple((jax.ShapeDtypeStruct(new.shape, F...  1.73 us

profile of v3, /device:TPU:32, one launch (start us, length us, event | category | flops | bytes accessed | tf_op | source)
XLA Modules:
  0.0 82.2 jit_solution(10635671605021970741)
XLA Ops:
  1.3 79.2 %swivel.1 = (f32[4,16,256]{2,1,0:T(8,128)}, f32[4,64,256]{2,1,0:T(8,128)}) custom-call(s32[1,1]{1,0:T(1,128)S(6)} %copy.9.count_ref, s32[2,8]{1,0:T(2,128)} %bitcast.3, f32[4,16,256]{2,1,0:T(8,128)} %row_ref.1, f32[4,64,256]{2,1,0:T(8,128)} %col_ref.1, bf16[4,16]{1,0:T(4,128)(2,1)} %rowm_ref.1, bf16[4,64]{1,0:T(4,128)(2,1)} %colm_ref.1, ...), custom_call_target="tpu_custom_call" | custom-call | flops 6400000000 | bytes 9000000 | tf_op jit(solution)/shard_map/swivel/pallas_call | solution.py:504
  80.5 1.7 %finish.1 = (f32[4,16,256]{2,1,0:T(8,128)}, f32[4,64,256]{2,1,0:T(8,128)}) custom-call(f32[4,16,256]{2,1,0:T(8,128)} %get-tuple-element.4.row_ref, f32[4,64,256]{2,1,0:T(8,128)} %get-tuple-element.5.col_ref), custom_call_target="tpu_custom_call" | custom-call | tf_op jit(solution)/shard_map/finish/pallas_call | solution.py:548

commit v4 on v3

--- a/solution.py
+++ b/solution.py
@@ -93,31 +93,26 @@
     def row_direct(p):
         mine = row_got_panel.at[p, core, 0, xh, pieces(p)]
         out = []
-        for n in (3, 4, 1, 2, 0):
-            for other in (0, 1):
-                if n == 0 and other == 0:
-                    continue
-                sem = n * 2 + other
-                there = row_got_panel.at[p, core, n, xh, pieces(p)]
-                side = xh if other == 0 else 1 - xh
-                here = row_got_panel.at[p, core, n, side, pieces(p)]
-                device = at_z(offset(n), other)
-                send = functools.partial(copy, mine, there, rp_s.at[p, sem], rp_r.at[p, sem], device)
-                recv = functools.partial(copy, here, here, rp_s.at[p, sem], rp_r.at[p, sem], device)
-                out.append((n, send, recv))
+        for n, other in ((3, 0), (4, 0), (3, 1), (4, 1), (1, 0), (2, 0), (0, 1), (1, 1), (2, 1)):
+            sem = n * 2 + other
+            there = row_got_panel.at[p, core, n, xh, pieces(p)]
+            side = xh if other == 0 else 1 - xh
+            here = row_got_panel.at[p, core, n, side, pieces(p)]
+            device = at_z(offset(n), other)
+            send = functools.partial(copy, mine, there, rp_s.at[p, sem], rp_r.at[p, sem], device)
+            recv = functools.partial(copy, here, here, rp_s.at[p, sem], rp_r.at[p, sem], device)
+            out.append(((n, other), send, recv))
         return out
 
-    def row_relay(p):
-        out = []
-        for sem, (src, dst, dz, side) in enumerate([(3, 5, 1, None), (4, 6, -1, None), (3, 7, 2, 0), (4, 7, -2, 1)]):
-            at = pl.ds(0, 2) if side is None else pl.ds(side, 1)
-            here = row_got_panel.at[p, core, src, at, pieces(p)]
-            there = row_got_panel.at[p, core, dst, at, pieces(p)]
-            out.append(copy(here, there, rp_s.at[p, 10 + sem], rp_r.at[p, 10 + sem], at_z(dz)))
-        return out
+    def row_relay(p, k):
+        src, dst, dz, other = ((3, 5, 1, 0), (3, 7, 2, 0), (4, 6, -1, 0), (3, 5, 1, 1), (4, 6, -1, 1), (4, 7, -2, 1))[k]
+        side = xh if other == 0 else 1 - xh
+        here = row_got_panel.at[p, core, src, side, pieces(p)]
+        there = row_got_panel.at[p, core, dst, side, pieces(p)]
+        return copy(here, there, rp_s.at[p, 10 + k], rp_r.at[p, 10 + k], at_z(dz))
 
     def row_hand(p, part, side):
-        slots = pl.ds(0, NEAR) if part == 0 else pl.ds(NEAR, 8 - NEAR)
+        slots = pl.ds(0, NEAR) if part == 0 else pl.ds(NEAR + part - 1, 1)
         block = row_got_panel.at[p, side, slots, :, pieces(p)]
         return copy(block, block, rf_s.at[p, part], rf_r.at[p, part], sibling)
 
@@ -168,38 +163,49 @@
         col_direct_got(p, 2).wait_recv()
         col_pass(p, 2).start()
 
-    def relay(p):
-        for n, _, recv in row_direct(p):
-            if n in (3, 4):
+    def row_direct_wait(p, *wanted):
+        for which, _, recv in row_direct(p):
+            if which in wanted:
                 recv().wait_recv()
-        for send in row_relay(p):
-            send.start()
+
+    def relay_own(p):
+        row_direct_wait(p, (3, 0))
+        row_relay(p, 0).start()
+        row_relay(p, 1).start()
+        row_direct_wait(p, (4, 0))
+        row_relay(p, 2).start()
+
+    def relay_other(p):
+        row_direct_wait(p, (3, 1))
+        row_relay(p, 3).start()
+        row_direct_wait(p, (4, 1))
+        row_relay(p, 4).start()
+        row_relay(p, 5).start()
 
     def hand_near(p):
-        for n, _, recv in row_direct(p):
-            if n not in (3, 4):
-                recv().wait_recv()
+        row_direct_wait(p, (1, 0), (1, 1), (2, 0), (2, 1), (0, 1))
         row_hand(p, 0, core).start()
 
     def hand_far(p):
-        for send in row_relay(p):
-            send.wait_recv()
-        row_hand(p, 1, core).start()
+        for part, relays in ((1, (0, 3)), (2, (2, 4)), (3, (1, 5))):
+            for k in relays:
+                row_relay(p, k).wait_recv()
+            row_hand(p, part, core).start()
 
     def gather_end(p):
         for q in (1, 3):
             col_direct_got(p, q).wait_recv()
         for q in ys:
             col_pass_got(p, q).wait_recv()
-        for part in range(2):
+        for part in range(4):
             row_hand(p, part, 1 - core).wait_recv()
 
     def gather_sent(p):
         for _, send, _ in row_direct(p):
             send().wait_send()
-        for send in row_relay(p):
-            send.wait_send()
-        for part in range(2):
+        for k in range(6):
+            row_relay(p, k).wait_send()
+        for part in range(4):
             row_hand(p, part, core).wait_send()
         for q in (NY,) + ys:
             col_direct(p, q).wait_send()
@@ -250,14 +256,15 @@
 
         lax.fori_loop(0, B // 64, part, 0)
 
-    loop(0, 4, prepare)
+    loop(0, 3, prepare)
+    relay_own(0)
+    prepare(3)
+    relay_other(0)
     pass_on(0)
+    pass_back(0)
     prepare(4)
-    pass_back(0)
-    prepare(5)
-    relay(0)
     hand_near(0)
-    loop(6, SLOTS, prepare)
+    loop(5, SLOTS, prepare)
     hand_far(0)
     gather_end(0)
     arrange(0)
@@ -315,16 +322,16 @@
 
     def far_sends(p):
         return [
+            copy(row_sum.at[7, 0], row_last.at[p, 0], rg_s.at[p, 12], rg_r.at[p, 12], at_z(2)),
+            copy(row_sum.at[7, 1], row_last.at[p, 1], rg_s.at[p, 13], rg_r.at[p, 13], at_z(-2)),
             copy(row_sum.at[5], row_far.at[p, 0], rg_s.at[p, 10], rg_r.at[p, 10], at_z(1)),
             copy(row_sum.at[6], row_far.at[p, 1], rg_s.at[p, 11], rg_r.at[p, 11], at_z(-1)),
-            copy(row_sum.at[7, 0], row_last.at[p, 0], rg_s.at[p, 12], rg_r.at[p, 12], at_z(2)),
-            copy(row_sum.at[7, 1], row_last.at[p, 1], rg_s.at[p, 13], rg_r.at[p, 13], at_z(-2)),
         ]
 
     def near_sends(p, slots):
         out = []
-        for m in slots:
-            for other in (0, 1):
+        for other in (1, 0):
+            for m in slots:
                 if m == 0 and other == 0:
                     continue
                 sem = m * 2 + other
@@ -402,27 +409,29 @@
             add(p, m)
         for send in near_sends(p, (1, 2, 0)):
             send.start()
-        for q in (1, 3):
-            col_part(xl * NY + lax.rem(y + q, NY))
-            straight_send(p, q).start()
-        col_part(r)
         cross_send(p, 2).wait_recv()
         col_add(p, xl * NY + lax.rem(y + 2, NY), (2,))
         straight_send(p, 2).start()
         for q in (1, 3):
-            cross_send(p, q).wait_recv()
-        col_add(p, across, (1, 3))
-        across_send(p).start()
-        for send in far_sends(p):
-            send.wait_recv()
-        for m, e in ((3, 0), (4, 1)):
+            col_part(xl * NY + lax.rem(y + q, NY))
+        col_part(r)
+        last_0, last_1, far_0, far_1 = far_sends(p)
+        for m, e, sends in ((3, 0, (far_0, last_0)), (4, 1, (far_1, last_1))):
+            for send in sends:
+                send.wait_recv()
             for side in range(2):
                 total = row_sum[m, side].astype(F32) + row_far[p, e, side].astype(F32)
                 if side == e:
                     total = total + row_last[p, e].astype(F32)
                 row_sum[m, side] = total.astype(BF16)
-        for send in near_sends(p, (3, 4)):
-            send.start()
+            for send in near_sends(p, (m,)):
+                send.start()
+        for q in (1, 3):
+            cross_send(p, q).wait_recv()
+        col_add(p, across, (1, 3))
+        across_send(p).start()
+        for q in (1, 3):
+            straight_send(p, q).start()
 
     def row_update(p):
         for send in near_sends(p, range(NEAR)):
@@ -461,9 +470,10 @@
     col_round(1)
     col_gather_send(1)
     scatter_sent(0)
+    relay_own(1)
+    relay_other(1)
     pass_on(1)
     pass_back(1)
-    relay(1)
     hand_near(1)
     hand_far(1)
     gather_end(1)
@@ -536,7 +546,7 @@
             pltpu.SMEM((16,), jnp.int32),
             pltpu.SMEM((SLOTS, 2), jnp.int32),
             dma((SLOTS,)), dma((2,)), dma((2,)),
-            dma((2, 14)), dma((2, 14)), dma((2, 2)), dma((2, 2)), dma((2, NROW)), dma((2, NROW)),
+            dma((2, 16)), dma((2, 16)), dma((2, 4)), dma((2, 4)), dma((2, NROW)), dma((2, NROW)),
             dma((2, 2)), dma((2, 2)), dma((2, 14)), dma((2, 14)), dma((2, NROW)), dma((2, NROW)),
         ],
         name="swivel",

time: 82.4 us -> 77.2 us (0.937)
  the two profiles are of different devices: /device:TPU:32 before, /device:TPU:1 now
where the time goes in v4:
time: 77.2 us; the launch traced here: 77.1 us
  Pallas kernels  75.8 us (98%)
  between operations  1.29 us (2%)
    pallas_call x1, Pallas kernels, shards(): pl.pallas_call(kernel, out_shape=(jax.ShapeDtypeStruct(row_emb.shape, F32...  74.1 us
    pallas_call x1, Pallas kernels, shards(): pl.pallas_call(finish, out_shape=tuple((jax.ShapeDtypeStruct(new.shape, F...  1.73 us

profile of v4, /device:TPU:1, one launch (start us, length us, event | category | flops | bytes accessed | tf_op | source)
XLA Modules:
  0.0 77.1 jit_solution(2412779741926856562)
XLA Ops:
  1.3 74.1 %swivel.1 = (f32[4,16,256]{2,1,0:T(8,128)}, f32[4,64,256]{2,1,0:T(8,128)}) custom-call(s32[1,1]{1,0:T(1,128)S(6)} %copy.9.count_ref, s32[2,8]{1,0:T(2,128)} %bitcast.3, f32[4,16,256]{2,1,0:T(8,128)} %row_ref.1, f32[4,64,256]{2,1,0:T(8,128)} %col_ref.1, bf16[4,16]{1,0:T(4,128)(2,1)} %rowm_ref.1, bf16[4,64]{1,0:T(4,128)(2,1)} %colm_ref.1, ...), custom_call_target="tpu_custom_call" | custom-call | flops 6400000000 | bytes 9000000 | tf_op jit(solution)/shard_map/swivel/pallas_call | solution.py:514
  75.4 1.7 %finish.1 = (f32[4,16,256]{2,1,0:T(8,128)}, f32[4,64,256]{2,1,0:T(8,128)}) custom-call(f32[4,16,256]{2,1,0:T(8,128)} %get-tuple-element.4.row_ref, f32[4,64,256]{2,1,0:T(8,128)} %get-tuple-element.5.col_ref), custom_call_target="tpu_custom_call" | custom-call | tf_op jit(solution)/shard_map/finish/pallas_call | solution.py:558

commit v5 on v4

--- a/solution.py
+++ b/solution.py
@@ -27,7 +27,7 @@
 def kernel(
     count_ref, list_ref, row_ref, col_ref, rowm_ref, colm_ref, data_ref, row_out, col_out, row_now, col_now,
     row_got_panel, col_panel, row_panel, tile_f32, picked, marg_left, marg_right, bias, weight,
-    stage, row_term, col_term, row_send, row_half, row_sum, row_far, row_last, row_got,
+    stage, signals, row_term, col_term, row_send, row_half, row_sum, row_far, row_last, row_got,
     col_send, col_cross, col_got, slot_of, pair_of,
     data_sem, in_sem, out_sem, rp_s, rp_r, rf_s, rf_r, cp_s, cp_r,
     sib_s, sib_r, rg_s, rg_r, cg_s, cg_r,
@@ -197,7 +197,10 @@
             col_direct_got(p, q).wait_recv()
         for q in ys:
             col_pass_got(p, q).wait_recv()
-        for part in range(4):
+        row_hand(p, 0, 1 - core).wait_recv()
+
+    def gather_far_end(p):
+        for part in range(1, 4):
             row_hand(p, part, 1 - core).wait_recv()
 
     def gather_sent(p):
@@ -212,7 +215,7 @@
         for q in ys:
             col_pass(p, q).wait_send()
 
-    def arrange(p):
+    def arrange(p, lo, hi):
         def slot(n):
             source = lax.rem(z - offset(n) + 2 * NZ, NZ)
             for side in range(2):
@@ -221,7 +224,7 @@
                     for i in range(4):
                         row_panel[i, rows, :] = row_got_panel[p, k, n, side, i]
 
-        loop(0, 8, slot)
+        loop(lo, hi, slot)
 
     col_round(0)
     row_round(0)
@@ -267,7 +270,7 @@
     loop(5, SLOTS, prepare)
     hand_far(0)
     gather_end(0)
-    arrange(0)
+    arrange(0, 0, NEAR)
 
     lane = lax.broadcasted_iota(jnp.int32, (ROWS, 128), 1)
     mine = lane == lax.broadcasted_iota(jnp.int32, (ROWS, 128), 0)
@@ -282,14 +285,17 @@
                     line = jnp.broadcast_to(margins[i : i + 1, 0:128], (ROWS, 128))
                     picked[i, rows, :] = jnp.where(mine, line, 0.0).astype(BF16)
 
-    loop(0, 8, pick)
-    ones = jnp.ones((128, 128), BF16)
-    for i in range(4):
-        marg_left[i] = jnp.dot(picked[i], ones, preferred_element_type=F32)
+    loop(0, NEAR, pick)
     for g in range(NROW // 2):
         low = col_panel[0, 2 * g, 16].astype(F32)[:, 0:128]
         high = col_panel[0, 2 * g + 1, 16].astype(F32)[:, 0:128]
         marg_right[:, g * 128 : (g + 1) * 128] = jnp.where(lane < COLS, low, pltpu.roll(high, COLS, 1))
+    gather_far_end(0)
+    arrange(0, NEAR, 8)
+    loop(NEAR, 8, pick)
+    ones = jnp.ones((128, 128), BF16)
+    for i in range(4):
+        marg_left[i] = jnp.dot(picked[i], ones, preferred_element_type=F32)
 
     def tiles(p):
         def tile(s):
@@ -306,11 +312,17 @@
             diff = scores.astype(BF16) + shift
             scale = weight[s]
             signal = jnp.where(scale > 0, scale * diff, 0.5 * jnp.tanh(0.5 * diff) + 0.5).astype(BF16)
+            signals[s] = signal
             row_term[s] = jnp.dot(signal, col_piece, preferred_element_type=F32)
-            col_term[s] = lax.dot_general(signal, row_piece, (((0,), (0,)), ((), ())), preferred_element_type=F32)
 
         for s in range(SLOTS):
             tile(s)
+
+    def col_terms(lo, hi):
+        for s in range(lo, hi):
+            col_term[s] = lax.dot_general(
+                signals[s], row_panel[pair_of[s, 0]], (((0,), (0,)), ((), ())), preferred_element_type=F32
+            )
 
     far, near = pl.ds(NEAR, 8 - NEAR), pl.ds(0, NEAR)
 
@@ -390,25 +402,27 @@
     def scatter(p):
         loop(NEAR, 8, row_part)
         sibling_send(p, 1).start()
-        col_part((1 - xl) * NY + lax.rem(y + 2, NY))
-        cross_send(p, 2).start()
         loop(0, NEAR, row_part)
         sibling_send(p, 0).start()
-        for q in (1, 3):
-            col_part((1 - xl) * NY + lax.rem(y + q, NY))
-            cross_send(p, q).start()
+        col_terms(0, 4)
         sibling_send(p, 1).wait_recv()
         for m in range(NEAR, 8):
             add(p, m)
         for send in far_sends(p):
             send.start()
-        col_part(xl * NY + lax.rem(y + 2, NY))
-        col_part(across)
+        col_terms(4, SLOTS)
+        col_part((1 - xl) * NY + lax.rem(y + 2, NY))
+        cross_send(p, 2).start()
+        for q in (1, 3):
+            col_part((1 - xl) * NY + lax.rem(y + q, NY))
+            cross_send(p, q).start()
         sibling_send(p, 0).wait_recv()
         for m in range(NEAR):
             add(p, m)
         for send in near_sends(p, (1, 2, 0)):
             send.start()
+        col_part(xl * NY + lax.rem(y + 2, NY))
+        col_part(across)
         cross_send(p, 2).wait_recv()
         col_add(p, xl * NY + lax.rem(y + 2, NY), (2,))
         straight_send(p, 2).start()
@@ -477,7 +491,9 @@
     hand_near(1)
     hand_far(1)
     gather_end(1)
-    arrange(1)
+    arrange(1, 0, NEAR)
+    gather_far_end(1)
+    arrange(1, NEAR, 8)
     tiles(1)
     scatter(1)
     row_update(1)
@@ -532,6 +548,7 @@
             pltpu.VMEM((SLOTS, B, B), BF16),
             pltpu.VMEM((SLOTS, B, B), BF16),
             pltpu.VMEM((SLOTS, B, B), jnp.int32),
+            pltpu.VMEM((SLOTS, B, B), BF16),
             pltpu.VMEM((SLOTS + 1, B, K), F32),
             pltpu.VMEM((SLOTS + 1, B, K), F32),
             pltpu.VMEM((2, 8, 2, 4, ROWS, K), BF16),

time: 77.2 us -> 80.3 us (1.040)
  the two profiles are of different devices: /device:TPU:1 before, /device:TPU:8 now
where the time goes in v5:
time: 80.3 us; the launch traced here: 80.2 us
  Pallas kernels  78.8 us (98%)
  between operations  1.45 us (2%)
    pallas_call x1, Pallas kernels, shards(): pl.pallas_call(kernel, out_shape=(jax.ShapeDtypeStruct(row_emb.shape, F32...  77 us
    pallas_call x1, Pallas kernels, shards(): pl.pallas_call(finish, out_shape=tuple((jax.ShapeDtypeStruct(new.shape, F...  1.73 us

profile of v5, /device:TPU:8, one launch (start us, length us, event | category | flops | bytes accessed | tf_op | source)
XLA Modules:
  0.0 80.2 jit_solution(8106249226971081150)
XLA Ops:
  1.3 77.0 %swivel.1 = (f32[4,16,256]{2,1,0:T(8,128)}, f32[4,64,256]{2,1,0:T(8,128)}) custom-call(s32[1,1]{1,0:T(1,128)S(6)} %copy.9.count_ref, s32[2,8]{1,0:T(2,128)} %bitcast.3, f32[4,16,256]{2,1,0:T(8,128)} %row_ref.1, f32[4,64,256]{2,1,0:T(8,128)} %col_ref.1, bf16[4,16]{1,0:T(4,128)(2,1)} %rowm_ref.1, bf16[4,64]{1,0:T(4,128)(2,1)} %colm_ref.1, ...), custom_call_target="tpu_custom_call" | custom-call | flops 6400000000 | bytes 9000000 | tf_op jit(solution)/shard_map/swivel/pallas_call | solution.py:530
  78.3 1.7 %finish.1 = (f32[4,16,256]{2,1,0:T(8,128)}, f32[4,64,256]{2,1,0:T(8,128)}) custom-call(f32[4,16,256]{2,1,0:T(8,128)} %get-tuple-element.4.row_ref, f32[4,64,256]{2,1,0:T(8,128)} %get-tuple-element.5.col_ref), custom_call_target="tpu_custom_call" | custom-call | tf_op jit(solution)/shard_map/finish/pallas_call | solution.py:575

commit v6 on v4

--- a/solution.py
+++ b/solution.py
@@ -27,7 +27,7 @@
 def kernel(
     count_ref, list_ref, row_ref, col_ref, rowm_ref, colm_ref, data_ref, row_out, col_out, row_now, col_now,
     row_got_panel, col_panel, row_panel, tile_f32, picked, marg_left, marg_right, bias, weight,
-    stage, row_term, col_term, row_send, row_half, row_sum, row_far, row_last, row_got,
+    stage, signals, row_term, col_term, row_send, row_half, row_sum, row_far, row_last, row_got,
     col_send, col_cross, col_got, slot_of, pair_of,
     data_sem, in_sem, out_sem, rp_s, rp_r, rf_s, rf_r, cp_s, cp_r,
     sib_s, sib_r, rg_s, rg_r, cg_s, cg_r,
@@ -306,11 +306,16 @@
             diff = scores.astype(BF16) + shift
             scale = weight[s]
             signal = jnp.where(scale > 0, scale * diff, 0.5 * jnp.tanh(0.5 * diff) + 0.5).astype(BF16)
-            row_term[s] = jnp.dot(signal, col_piece, preferred_element_type=F32)
+            signals[s] = signal
             col_term[s] = lax.dot_general(signal, row_piece, (((0,), (0,)), ((), ())), preferred_element_type=F32)
 
         for s in range(SLOTS):
             tile(s)
+
+    def row_terms(p):
+        for s in range(SLOTS):
+            col_piece = col_panel[p, :, pl.ds(4 * pair_of[s, 1], 4)].reshape(B, K)
+            row_term[s] = jnp.dot(signals[s], col_piece, preferred_element_type=F32)
 
     far, near = pl.ds(NEAR, 8 - NEAR), pl.ds(0, NEAR)
 
@@ -388,15 +393,16 @@
             col_send[t, j] = total.astype(BF16)
 
     def scatter(p):
-        loop(NEAR, 8, row_part)
-        sibling_send(p, 1).start()
         col_part((1 - xl) * NY + lax.rem(y + 2, NY))
         cross_send(p, 2).start()
-        loop(0, NEAR, row_part)
-        sibling_send(p, 0).start()
         for q in (1, 3):
             col_part((1 - xl) * NY + lax.rem(y + q, NY))
             cross_send(p, q).start()
+        row_terms(p)
+        loop(NEAR, 8, row_part)
+        sibling_send(p, 1).start()
+        loop(0, NEAR, row_part)
+        sibling_send(p, 0).start()
         sibling_send(p, 1).wait_recv()
         for m in range(NEAR, 8):
             add(p, m)
@@ -532,6 +538,7 @@
             pltpu.VMEM((SLOTS, B, B), BF16),
             pltpu.VMEM((SLOTS, B, B), BF16),
             pltpu.VMEM((SLOTS, B, B), jnp.int32),
+            pltpu.VMEM((SLOTS, B, B), BF16),
             pltpu.VMEM((SLOTS + 1, B, K), F32),
             pltpu.VMEM((SLOTS + 1, B, K), F32),
             pltpu.VMEM((2, 8, 2, 4, ROWS, K), BF16),

time: 77.2 us -> 79.1 us (1.025)
  Pallas kernels: 75.8 us -> 77.7 us
    pallas_call x1, Pallas kernels: 74.1 us -> 76 us  [shards(): pl.pallas_call(kernel, out_shape=(jax.ShapeDtypeStruct(row_emb.shape, F32...]
where the time goes in v6:
time: 79.1 us; the launch traced here: 79 us
  Pallas kernels  77.7 us (98%)
  between operations  1.29 us (2%)
    pallas_call x1, Pallas kernels, shards(): pl.pallas_call(kernel, out_shape=(jax.ShapeDtypeStruct(row_emb.shape, F32...  76 us
    pallas_call x1, Pallas kernels, shards(): pl.pallas_call(finish, out_shape=tuple((jax.ShapeDtypeStruct(new.shape, F...  1.73 us

profile of v6, /device:TPU:1, one launch (start us, length us, event | category | flops | bytes accessed | tf_op | source)
XLA Modules:
  0.0 79.0 jit_solution(1146619335968748853)
XLA Ops:
  1.3 76.0 %swivel.1 = (f32[4,16,256]{2,1,0:T(8,128)}, f32[4,64,256]{2,1,0:T(8,128)}) custom-call(s32[1,1]{1,0:T(1,128)S(6)} %copy.9.count_ref, s32[2,8]{1,0:T(2,128)} %bitcast.3, f32[4,16,256]{2,1,0:T(8,128)} %row_ref.1, f32[4,64,256]{2,1,0:T(8,128)} %col_ref.1, bf16[4,16]{1,0:T(4,128)(2,1)} %rowm_ref.1, bf16[4,64]{1,0:T(4,128)(2,1)} %colm_ref.1, ...), custom_call_target="tpu_custom_call" | custom-call | flops 6400000000 | bytes 9000000 | tf_op jit(solution)/shard_map/swivel/pallas_call | solution.py:520
  77.3 1.7 %finish.1 = (f32[4,16,256]{2,1,0:T(8,128)}, f32[4,64,256]{2,1,0:T(8,128)}) custom-call(f32[4,16,256]{2,1,0:T(8,128)} %get-tuple-element.4.row_ref, f32[4,64,256]{2,1,0:T(8,128)} %get-tuple-element.5.col_ref), custom_call_target="tpu_custom_call" | custom-call | tf_op jit(solution)/shard_map/finish/pallas_call | solution.py:565
